TPU v7x, 128 devices: a whole 4x4x4 slice. The times are simulated.
128 devices in a mesh: dp: 8 (over x_hi, z), fsdp: 16 (over y, x_lo, core).
Axes of the slice: x: 4 (x_hi: 2, x_lo: 2; x = x_hi * 2 + x_lo), y: 4, z: 4, core: 2. Of those that a mesh axis runs over, the one named last changes fastest.
Arguments:
- queries: bfloat16 [36864, 3072], P(('dp', 'fsdp')), may hold values from -8 to 8
- key_vectors: bfloat16 [36864, 3072], P(('dp', 'fsdp')), may hold values from -8 to 8
- value_vectors: bfloat16 [36864, 3072], P(('dp', 'fsdp')), may hold values from -6 to 6
- image_lengths: int32 [128, 6], replicated, may hold values from 16 to 208, as said below
- image_dest: int32 [128, 6], replicated, may hold values from 0 to 7, as said below
- image_offset: int32 [128, 6], replicated, may hold values from 0 to 272, as said below
- out_weight: bfloat16 [3072, 3072], P('fsdp'), may hold values from -0.109375 to 0.109375
- out_grad: bfloat16 [36864, 3072], P(('dp', 'fsdp')), may hold values from -24 to 24
Outputs:
- projected: bfloat16 [36864, 3072], P(('dp', 'fsdp'))
- query_grad: bfloat16 [36864, 3072], P(('dp', 'fsdp'))
- key_grad: bfloat16 [36864, 3072], P(('dp', 'fsdp'))
- value_grad: bfloat16 [36864, 3072], P(('dp', 'fsdp'))
- weight_grad: bfloat16 [3072, 3072], P('fsdp', 'dp')
Inputs may be any that keep to these rules, and one draw needn't show every extreme that they name: `image_lengths`: every length is a multiple of 16; the lengths of one device sum to 288; every device holds at least three images of exactly 16 patches; in each group of devices that share an fsdp index, at least one device holds an image of exactly 208 patches. `image_dest`: A device's image keeps its dp index or moves to another device with the same fsdp index. Each device sends exactly three images, each of 16 patches, to three different devices, and receives three such images. `image_offset`: offsets are multiples of 16; the images that land on one device, kept and received, cover its 288 rows exactly, without intersection.
All inputs are finite; a program needn't handle non-finite values.
Results may differ from a plain program's by a relative error of at most 0.025.
Values may be sent and summed in bfloat16 or wider, within the bound.
A program may use at most 192 MiB of HBM per device.

v0:
```python
import jax
import jax.numpy as jnp
from jax import lax
from jax.sharding import PartitionSpec as P

HD = 128
SLOT = 16


def attention(query_rows, key_rows, value_rows, same_image):
    row_count = query_rows.shape[0]
    head_count = query_rows.shape[1] // HD
    query_heads = query_rows.reshape(row_count, head_count, HD).astype(jnp.float32)
    key_heads = key_rows.reshape(row_count, head_count, HD).astype(jnp.float32)
    value_heads = value_rows.reshape(row_count, head_count, HD).astype(jnp.float32)
    scores = jnp.einsum("ahd,bhd->hab", query_heads, key_heads) * HD ** (-0.5)
    scores = jnp.where(same_image[None, :, :], scores, -1e30)
    row_max = lax.stop_gradient(jnp.max(scores, axis=2, keepdims=True))
    powers = jnp.exp(scores - row_max)
    weights = (powers / jnp.sum(powers, axis=2, keepdims=True)).astype(jnp.bfloat16)
    mixed = jnp.einsum("hab,bhd->ahd", weights.astype(jnp.float32), value_heads)
    return mixed.reshape(row_count, head_count * HD).astype(jnp.bfloat16)


def select_row(table, index):
    return lax.dynamic_index_in_dim(table, index, axis=0, keepdims=False)


def take_slots(matrix, slot_source, slot_valid):
    taken = jnp.take(matrix, slot_source.reshape(-1), axis=0).reshape(
        slot_source.shape[0], slot_source.shape[1], matrix.shape[1]
    )
    return jnp.where(slot_valid[:, :, None], taken, jnp.zeros((), matrix.dtype))


def from_pool(local_rows, arrived, row_source):
    pooled = jnp.concatenate(
        [local_rows, arrived.reshape(arrived.shape[0] * arrived.shape[1], arrived.shape[2])], axis=0
    )
    return jnp.take(pooled, row_source, axis=0)


def shards(
    queries,
    key_vectors,
    value_vectors,
    image_lengths,
    image_dest,
    image_offset,
    out_weight,
    out_grad,
):
    row_count = queries.shape[0]
    img_count = image_lengths.shape[1]
    dp_count = lax.axis_size("dp")
    fs_count = lax.axis_size("fsdp")
    dp_index = lax.axis_index("dp")
    fs_index = lax.axis_index("fsdp")
    starts = jnp.cumsum(image_lengths, axis=1) - image_lengths

    def group_view(table):
        return lax.dynamic_index_in_dim(
            table.reshape(dp_count, fs_count, img_count), fs_index, axis=1, keepdims=False
        )

    grp_len = group_view(image_lengths)
    grp_start = group_view(starts)
    grp_dest = group_view(image_dest)
    grp_off = group_view(image_offset)
    own_len = select_row(grp_len, dp_index)
    own_start = select_row(grp_start, dp_index)
    own_dest = select_row(grp_dest, dp_index)
    own_off = select_row(grp_off, dp_index)
    peers = jnp.arange(dp_count, dtype=jnp.int32)
    slot_ids = jnp.arange(SLOT, dtype=jnp.int32)
    row_ids = jnp.arange(row_count, dtype=jnp.int32)
    leaving = (own_dest[None, :] == peers[:, None]) & (own_dest[None, :] != dp_index)
    send_source = (
        jnp.sum(jnp.where(leaving, own_start[None, :], 0), axis=1)[:, None] + slot_ids[None, :]
    )
    send_valid = (
        jnp.sum(
            jnp.where(
                leaving[:, :, None] & (slot_ids[None, None, :] < own_len[None, :, None]), 1, 0
            ),
            axis=1,
        )
        > 0
    )
    got_q, got_k, got_v = (
        lax.all_to_all(
            take_slots(queries, send_source, send_valid),
            "dp",
            split_axis=0,
            concat_axis=0,
            tiled=True,
        ),
        lax.all_to_all(
            take_slots(key_vectors, send_source, send_valid),
            "dp",
            split_axis=0,
            concat_axis=0,
            tiled=True,
        ),
        lax.all_to_all(
            take_slots(value_vectors, send_source, send_valid),
            "dp",
            split_axis=0,
            concat_axis=0,
            tiled=True,
        ),
    )
    senders = peers[:, None]
    arriving = grp_dest == dp_index
    source_base = jnp.where(senders == dp_index, grp_start, row_count + senders * SLOT) - grp_off
    covers = (
        arriving[:, :, None]
        & (row_ids[None, None, :] >= grp_off[:, :, None])
        & (row_ids[None, None, :] < (grp_off + grp_len)[:, :, None])
    )
    row_source = jnp.sum(
        jnp.where(covers, source_base[:, :, None] + row_ids[None, None, :], 0), axis=(0, 1)
    )
    image_ids = senders * img_count + jnp.arange(img_count, dtype=jnp.int32)[None, :]
    segment = jnp.sum(jnp.where(covers, image_ids[:, :, None], 0), axis=(0, 1))
    moved_q = from_pool(queries, got_q, row_source)
    moved_k = from_pool(key_vectors, got_k, row_source)
    moved_v = from_pool(value_vectors, got_v, row_source)
    same_image = segment[:, None] == segment[None, :]
    attn, pullback = jax.vjp(
        lambda first_in, second_in, third_in: attention(first_in, second_in, third_in, same_image),
        moved_q,
        moved_k,
        moved_v,
    )
    full_weight = lax.all_gather(out_weight, "fsdp", axis=0, tiled=True)
    projected = jnp.dot(attn, full_weight, preferred_element_type=jnp.float32)
    attn_grad = lax.dot_general(
        out_grad, full_weight, (((1,), (1,)), ((), ())), preferred_element_type=jnp.float32
    ).astype(jnp.bfloat16)
    grad_q, grad_k, grad_v = pullback(attn_grad)
    grad_scale = (row_count * dp_count * fs_count) ** (-0.5)
    weight_shard = lax.psum_scatter(
        (
            lax.dot_general(
                attn, out_grad, (((0,), (0,)), ((), ())), preferred_element_type=jnp.float32
            )
            * grad_scale
        ).astype(jnp.bfloat16),
        "fsdp",
        scatter_dimension=0,
        tiled=True,
    )
    weight_grad = lax.psum_scatter(weight_shard, "dp", scatter_dimension=1, tiled=True)
    returning = arriving & (senders != dp_index)
    back_source = jnp.sum(jnp.where(returning, grp_off, 0), axis=1)[:, None] + slot_ids[None, :]
    back_valid = (
        jnp.sum(
            jnp.where(
                returning[:, :, None] & (slot_ids[None, None, :] < grp_len[:, :, None]), 1, 0
            ),
            axis=1,
        )
        > 0
    )
    home_q, home_k, home_v = (
        lax.all_to_all(
            take_slots(grad_q, back_source, back_valid),
            "dp",
            split_axis=0,
            concat_axis=0,
            tiled=True,
        ),
        lax.all_to_all(
            take_slots(grad_k, back_source, back_valid),
            "dp",
            split_axis=0,
            concat_axis=0,
            tiled=True,
        ),
        lax.all_to_all(
            take_slots(grad_v, back_source, back_valid),
            "dp",
            split_axis=0,
            concat_axis=0,
            tiled=True,
        ),
    )
    stays = own_dest == dp_index
    home_base = jnp.where(stays, own_off, row_count + own_dest * SLOT) - own_start
    inside = (row_ids[None, :] >= own_start[:, None]) & (
        row_ids[None, :] < (own_start + own_len)[:, None]
    )
    home_source = jnp.sum(jnp.where(inside, home_base[:, None] + row_ids[None, :], 0), axis=0)
    query_grad = from_pool(grad_q, home_q, home_source)
    key_grad = from_pool(grad_k, home_k, home_source)
    value_grad = from_pool(grad_v, home_v, home_source)
    return (projected.astype(jnp.bfloat16), query_grad, key_grad, value_grad, weight_grad)


def solution(mesh):
    in_specs = (
        P(("dp", "fsdp"), None),
        P(("dp", "fsdp"), None),
        P(("dp", "fsdp"), None),
        P(),
        P(),
        P(),
        P("fsdp", None),
        P(("dp", "fsdp"), None),
    )
    out_specs = (
        P(("dp", "fsdp"), None),
        P(("dp", "fsdp"), None),
        P(("dp", "fsdp"), None),
        P(("dp", "fsdp"), None),
        P("fsdp", "dp"),
    )
    return jax.shard_map(shards, mesh=mesh, in_specs=in_specs, out_specs=out_specs, check_vma=False)
```

profile of v0, /device:TPU:1, one launch (start us, length us, event | category | flops | bytes accessed | tf_op | source)
XLA Modules:
  0.0 497.7 jit_solution(239722224310865682)
XLA Ops:
  17.3 4.7 gather_fusion.4
  24.0 4.7 gather_fusion
  34.0 8.4 %all-to-all-start.1 = ((bf16[8,16,3072]{2,1,0:T(8,128)(2,1)}), bf16[8,16,3072]{2,1,0:T(8,128)(2,1)}, u32[]{:S(2)}, u32[]{:S(2)}) async-start(bf16[8,16,3072]{2,1,0:T(8,128)(2,1)} %get-tuple-element.19), calls=%async_computation.1 | async-start | bytes 1572864 | tf_op jit(solution)/shard_map/all_to_all | solution.py:91
  47.0 16.2 %all-to-all-done.1 = bf16[8,16,3072]{2,1,0:T(8,128)(2,1)} async-done(((bf16[8,16,3072]{2,1,0:T(8,128)(2,1)}), bf16[8,16,3072]{2,1,0:T(8,128)(2,1)}, u32[]{:S(2)}, u32[]{:S(2)}) %all-to-all-start.1) | async-done | bytes 786464 | tf_op jit(solution)/shard_map/all_to_all | solution.py:91
  63.2 4.2 all-to-all-start.2
  70.2 17.7 %all-to-all-done.2 = bf16[8,16,3072]{2,1,0:T(8,128)(2,1)} async-done(((bf16[8,16,3072]{2,1,0:T(8,128)(2,1)}), bf16[8,16,3072]{2,1,0:T(8,128)(2,1)}, u32[]{:S(2)}, u32[]{:S(2)}) %all-to-all-start.2) | async-done | bytes 786464 | tf_op jit(solution)/shard_map/all_to_all | solution.py:98
  95.2 8.9 %gather_fusion.5 = bf16[288,3072]{1,0:T(8,128)(2,1)} fusion(bf16[416,3072]{1,0:T(8,128)(2,1)} %pad_maximum_fusion.2, s32[1024]{0:T(1024)S(1)} %pad_clamp_fusion.2), kind=kCustom, calls=%fused_computation.8.clone | custom fusion | bytes 3540096 | tf_op jit(solution)/shard_map/jit(_take)/gather | solution.py:40
  106.9 8.9 %gather_fusion.3 = bf16[288,3072]{1,0:T(8,128)(2,1)} fusion(bf16[416,3072]{1,0:T(8,128)(2,1)} %pad_maximum_fusion.1, s32[1024]{0:T(1024)S(1)} %pad_clamp_fusion.2), kind=kCustom, calls=%fused_computation.7.clone | custom fusion | bytes 3540096 | tf_op jit(solution)/shard_map/jit(_take)/gather | solution.py:40
  118.6 9.2 %gather_fusion.1 = bf16[288,3072]{1,0:T(8,128)(2,1)} fusion(bf16[416,3072]{1,0:T(8,128)(2,1)} %pad_maximum_fusion, s32[1024]{0:T(1024)S(1)} %pad_clamp_fusion.2), kind=kCustom, calls=%fused_computation.1.clone | custom fusion | bytes 3540096 | tf_op jit(solution)/shard_map/jit(_take)/gather | solution.py:40
  133.5 5.5 %fusion.16 = f32[24,288,288]{1,2,0:T(8,128)} fusion(bf16[36,24,8,128]{3,2,1,0:T(8,128)(2,1)S(1)} %get-tuple-element.31, bf16[36,24,8,128]{3,2,1,0:T(8,128)(2,1)S(1)} %get-tuple-element.30), kind=kOutput, calls=%fused_computation.47 | convolution fusion | flops 509607936 | bytes 11501568 | tf_op jit(solution)/shard_map/jvp(ahd,bhd->hab)/dot_general | solution.py:16
  139.0 15.2 %fusion.54 = (f32[24,288]{1,0:T(8,128)S(1)}, f32[24,288,288]{1,2,0:T(8,128)}) fusion(f32[24,288,288]{1,2,0:T(8,128)} %fusion.16, pred[288,288]{0,1:T(8,128)(4,1)S(1)} %copy-done.28), kind=kOutput, calls=%fused_computation.149 | output fusion | flops 11944223 | bytes 16035840 | tf_op jit(solution)/shard_map/jvp()/sub | solution.py:19
  155.4 9.9 %fusion.40 = bf16[36,24,8,128]{3,2,1,0:T(8,128)(2,1)S(1)} fusion(bf16[288,3072]{1,0:T(8,128)(2,1)S(1)} %copy-done, bf16[3072,3072]{1,0:T(8,128)(2,1)} %all-gather.2.cloned.1.call-done), kind=kOutput, calls=%fused_computation.75 | convolution fusion | flops 5436702720 | bytes 22413312 | tf_op jit(solution)/shard_map/dot_general | solution.py:138
  165.4 8.2 %fusion.6 = (f32[24,288]{1,0:T(8,128)}, bf16[24,288,288]{1,2,0:T(8,128)(2,1)S(1)}, bf16[24,288,288]{1,2,0:T(8,128)(2,1)}) fusion(f32[24,288,288]{1,2,0:T(8,128)} %get-tuple-element.36, f32[24,288]{1,0:T(8,128)S(1)} %copy-done.35, f32[24,288]{1,0:T(8,128)S(1)} %copy-done.31, bf16[36,24,8,128]{3,2,1,0:T(8,128)(2,1)S(1)} %copy-done.13, ...), kind=kOutput, calls=%fused_computation.21 | convolution fusion | flops 523535616 | bytes 19547136 | tf_op jit(solution)/shard_map/transpose(jvp(hab,bhd->ahd))/dot_general | solution.py:21
  179.1 13.3 %multiply_convert_fusion = bf16[3072,3072]{1,0:T(8,128)(2,1)} fusion(bf16[288,3072]{1,0:T(8,128)(2,1)S(1)} %copy-done, bf16[24,36,8,128]{3,2,1,0:T(8,128)(2,1)S(1)} %convert_bitcast_fusion.3), kind=kOutput, calls=%fused_computation.13 | convolution fusion | flops 5454692352 | bytes 22413312 | tf_op jit(solution)/shard_map/dot_general | solution.py:145
  199.7 10.6 %convert_bitcast_fusion.2 = bf16[24,36,8,128]{3,2,1,0:T(8,128)(2,1)} fusion(bf16[36,24,8,128]{3,2,1,0:T(8,128)(2,1)S(1)} %copy-done.12, f32[24,288,288]{1,2,0:T(8,128)} %get-tuple-element.36, bf16[24,288,288]{1,2,0:T(8,128)(2,1)} %get-tuple-element.37, f32[24,288]{1,0:T(8,128)} %neg.6, f32[24,288]{1,0:T(8,128)} %copy-done.30, ...), kind=kOutput, calls=%fused_computation.60 | convolution fusion | flops 522436608 | bytes 15621120 | tf_op jit(solution)/shard_map/transpose(jvp(ahd,bhd->hab))/dot_general | solution.py:16
  212.6 9.5 %convert_bitcast_fusion.1 = bf16[24,36,8,128]{3,2,1,0:T(8,128)(2,1)S(1)} fusion(bf16[36,24,8,128]{3,2,1,0:T(8,128)(2,1)S(1)} %copy-done.10, f32[24,288,288]{1,2,0:T(8,128)} %get-tuple-element.36, bf16[24,288,288]{1,2,0:T(8,128)(2,1)} %get-tuple-element.37, f32[24,288]{1,0:T(8,128)S(1)} %copy-done.34, f32[24,288]{1,0:T(8,128)S(1)} %copy-done.32, ...), kind=kOutput, calls=%fused_computation.59 | convolution fusion | flops 522436608 | bytes 15621120 | tf_op jit(solution)/shard_map/transpose(jvp(ahd,bhd->hab))/dot_general | solution.py:16
  223.8 4.5 gather_fusion.8
  235.3 5.8 %all-to-all-start.5 = ((bf16[8,16,3072]{2,1,0:T(8,128)(2,1)}), bf16[8,16,3072]{2,1,0:T(8,128)(2,1)S(1)}, u32[]{:S(2)}, u32[]{:S(2)}) async-start(bf16[8,16,3072]{2,1,0:T(8,128)(2,1)} %get-tuple-element.15), calls=%async_computation.5 | async-start | bytes 1572864 | tf_op jit(solution)/shard_map/all_to_all | solution.py:181
  241.2 165.0 %reduce-scatter.5.cloned.1.call-done = bf16[192,3072]{1,0:T(8,128)(2,1)} async-done(((bf16[3072,3072]{1,0:T(8,128)(2,1)}), bf16[192,3072]{1,0:T(8,128)(2,1)}) %reduce-scatter.5.cloned.1.call-update) | async-done | bytes 1179664 | tf_op jit(solution)/shard_map/reduce_scatter | solution.py:143
  408.7 6.3 %all-to-all-start.4 = ((bf16[8,16,3072]{2,1,0:T(8,128)(2,1)}), bf16[8,16,3072]{2,1,0:T(8,128)(2,1)S(1)}, u32[]{:S(2)}, u32[]{:S(2)}) async-start(bf16[8,16,3072]{2,1,0:T(8,128)(2,1)} %get-tuple-element.16), calls=%async_computation.4 | async-start | bytes 1572864 | tf_op jit(solution)/shard_map/all_to_all | solution.py:174
  415.0 11.0 %convolution_convert_fusion.1 = bf16[288,3072]{1,0:T(8,128)(2,1)} fusion(bf16[3072,3072]{1,0:T(8,128)(2,1)} %all-gather.2.cloned.1.call-done, bf16[24,36,8,128]{3,2,1,0:T(8,128)(2,1)S(1)} %copy-done.22), kind=kOutput, calls=%fused_computation.30 | convolution fusion | flops 5436702720 | bytes 22413312 | tf_op jit(solution)/shard_map/dot_general | solution.py:137
  426.3 6.3 %all-to-all-start.3 = ((bf16[8,16,3072]{2,1,0:T(8,128)(2,1)}), bf16[8,16,3072]{2,1,0:T(8,128)(2,1)}, u32[]{:S(2)}, u32[]{:S(2)}) async-start(bf16[8,16,3072]{2,1,0:T(8,128)(2,1)} %get-tuple-element.17), calls=%async_computation.3 | async-start | bytes 1572864 | tf_op jit(solution)/shard_map/all_to_all | solution.py:167
  449.1 5.3 %broadcast_select_fusion = (bf16[288,3072]{1,0:T(8,128)(2,1)}, bf16[288,3072]{1,0:T(8,128)(2,1)}, bf16[288,3072]{1,0:T(8,128)(2,1)}) fusion(bf16[288,3072]{1,0:T(8,128)(2,1)} %gather_fusion.11, pred[288]{0:T(512)(128)(4,1)S(1)} %copy-done.40, bf16[288,3072]{1,0:T(8,128)(2,1)} %gather_fusion.9, bf16[288,3072]{1,0:T(8,128)(2,1)} %gather_fusion.7), kind=kLoop, calls=%fused_computation.62 | loop fusion | flops 2654208 | bytes 10617120 | tf_op jit(solution)/shard_map/jit(_take)/select_n | solution.py:40
  454.4 34.8 %reduce-scatter.7.cloned.1.call-done = bf16[384,192]{1,0:T(8,128)(2,1)} async-done(((bf16[3072,192]{1,0:T(8,128)(2,1)}), bf16[384,192]{1,0:T(8,128)(2,1)}) %reduce-scatter.7.cloned.1.call-update) | async-done | bytes 147472
  (195 shorter events, 89.1 us)
Async XLA Ops:
  7.2 148.3 %copy-start = (bf16[288,3072]{1,0:T(8,128)(2,1)S(1)}, bf16[288,3072]{1,0:T(8,128)(2,1)}, u32[]{:S(2)}) copy-start(bf16[288,3072]{1,0:T(8,128)(2,1)} %param.19) | copy-start | bytes 5308420
  7.2 148.2 %all-gather.2.cloned.1.call-start = ((), (), s32[]{:S(2)}) async-start(), calls=%async_computation.8 | async-start | bytes 20054016 | tf_op jit(solution)/shard_map/all_gather | solution.py:136
  8.7 8.0 %copy-start.26 = (s32[8,16,6]{1,0,2:T(8,128)}, s32[8,16,6]{1,0,2:T(8,128)S(1)}, u32[]{:S(2)}) copy-start(s32[8,16,6]{1,0,2:T(8,128)S(1)} %reshape.376) | copy-start | bytes 9220
  34.0 58.4 %copy-start.4 = (bf16[288,3072]{1,0:T(8,128)(2,1)S(1)}, bf16[288,3072]{1,0:T(8,128)(2,1)}, u32[]{:S(2)}) copy-start(bf16[288,3072]{1,0:T(8,128)(2,1)} %param.13) | copy-start | bytes 5308420
  34.0 29.3 %all-to-all-start.1 = ((bf16[8,16,3072]{2,1,0:T(8,128)(2,1)}), bf16[8,16,3072]{2,1,0:T(8,128)(2,1)}, u32[]{:S(2)}, u32[]{:S(2)}) async-start(bf16[8,16,3072]{2,1,0:T(8,128)(2,1)} %get-tuple-element.19), calls=%async_computation.1 | async-start | bytes 1572864 | tf_op jit(solution)/shard_map/all_to_all | solution.py:91
  63.2 24.7 %all-to-all-start.2 = ((bf16[8,16,3072]{2,1,0:T(8,128)(2,1)}), bf16[8,16,3072]{2,1,0:T(8,128)(2,1)}, u32[]{:S(2)}, u32[]{:S(2)}) async-start(bf16[8,16,3072]{2,1,0:T(8,128)(2,1)} %get-tuple-element.20), calls=%async_computation.2 | async-start | bytes 1572864 | tf_op jit(solution)/shard_map/all_to_all | solution.py:98
  87.9 27.9 %all-to-all-start = ((bf16[8,16,3072]{2,1,0:T(8,128)(2,1)}), bf16[8,16,3072]{2,1,0:T(8,128)(2,1)}, u32[]{:S(2)}, u32[]{:S(2)}) async-start(bf16[8,16,3072]{2,1,0:T(8,128)(2,1)} %get-tuple-element.18), calls=%async_computation | async-start | bytes 1572864 | tf_op jit(solution)/shard_map/all_to_all | solution.py:105
  92.1 314.0 %reduce-scatter.5.cloned.1.call-start = ((), (), s32[]{:S(2)}) async-start(), calls=%async_computation.9 | async-start | bytes 20054016 | tf_op jit(solution)/shard_map/reduce_scatter | solution.py:143
  95.2 8.9 %copy-start.6 = (bf16[288,3072]{1,0:T(8,128)(2,1)S(1)}, bf16[288,3072]{1,0:T(8,128)(2,1)}, u32[]{:S(2)}) copy-start(bf16[288,3072]{1,0:T(8,128)(2,1)} %param.12) | copy-start | bytes 5308420
  106.9 8.9 %copy-start.7 = (bf16[288,3072]{1,0:T(8,128)(2,1)S(1)}, bf16[288,3072]{1,0:T(8,128)(2,1)}, u32[]{:S(2)}) copy-start(bf16[288,3072]{1,0:T(8,128)(2,1)} %param.14) | copy-start | bytes 5308420
  118.6 9.3 %copy-start.8 = (bf16[288,3072]{1,0:T(8,128)(2,1)S(1)}, bf16[288,3072]{1,0:T(8,128)(2,1)}, u32[]{:S(2)}) copy-start(bf16[288,3072]{1,0:T(8,128)(2,1)} %gather_fusion.5) | copy-start | bytes 5308420
  118.6 9.3 %copy-start.41 = (pred[288]{0:T(512)(128)(4,1)S(1)}, pred[288]{0:T(512)(128)(4,1)}, u32[]{:S(2)}) copy-start(pred[288]{0:T(512)(128)(4,1)} %get-tuple-element.39) | copy-start | bytes 868
  155.4 10.0 %copy-start.13 = (bf16[36,24,8,128]{3,2,1,0:T(8,128)(2,1)S(1)}, bf16[36,24,8,128]{3,2,1,0:T(8,128)(2,1)}, u32[]{:S(2)}) copy-start(bf16[36,24,8,128]{3,2,1,0:T(8,128)(2,1)} %get-tuple-element.29) | copy-start | bytes 5308420
  155.4 10.0 %copy-start.31 = (f32[24,288]{1,0:T(8,128)S(1)}, f32[24,288]{1,0:T(8,128)}, u32[]{:S(2)}) copy-start(f32[24,288]{1,0:T(8,128)} %copy-done.30) | copy-start | bytes 82948
  155.4 10.0 %copy-start.35 = (f32[24,288]{1,0:T(8,128)S(1)}, f32[24,288]{1,0:T(8,128)}, u32[]{:S(2)}) copy-start(f32[24,288]{1,0:T(8,128)} %multiply_divide_fusion) | copy-start | bytes 82948
  165.4 8.2 %copy-start.48 = (bf16[36,24,8,128]{3,2,1,0:T(8,128)(2,1)}, bf16[36,24,8,128]{3,2,1,0:T(8,128)(2,1)S(1)}, u32[]{:S(2)}) copy-start(bf16[36,24,8,128]{3,2,1,0:T(8,128)(2,1)S(1)} %fusion.40) | copy-start | bytes 5308420
  198.7 31.5 %copy-start.3 = (bf16[24,36,8,128]{3,2,0,1:T(8,128)(2,1)}, bf16[24,36,8,128]{3,2,0,1:T(8,128)(2,1)S(1)}, u32[]{:S(2)}) copy-start(bf16[24,36,8,128]{3,2,0,1:T(8,128)(2,1)S(1)} %copy.159) | copy-start | bytes 5308420
  212.6 15.7 %copy-start.2 = (bf16[24,36,8,128]{3,2,0,1:T(8,128)(2,1)}, bf16[24,36,8,128]{3,2,0,1:T(8,128)(2,1)S(1)}, u32[]{:S(2)}) copy-start(bf16[24,36,8,128]{3,2,0,1:T(8,128)(2,1)S(1)} %copy.161) | copy-start | bytes 5308420
  235.3 173.5 %all-to-all-start.5 = ((bf16[8,16,3072]{2,1,0:T(8,128)(2,1)}), bf16[8,16,3072]{2,1,0:T(8,128)(2,1)S(1)}, u32[]{:S(2)}, u32[]{:S(2)}) async-start(bf16[8,16,3072]{2,1,0:T(8,128)(2,1)} %get-tuple-element.15), calls=%async_computation.5 | async-start | bytes 1572864 | tf_op jit(solution)/shard_map/all_to_all | solution.py:181
  241.1 248.1 %reduce-scatter.7.cloned.1.call-start = ((), (), s32[]{:S(2)}) async-start(), calls=%async_computation.10 | async-start | bytes 1769472
  241.2 173.8 %copy-start.22 = (bf16[24,36,8,128]{3,2,1,0:T(8,128)(2,1)S(1)}, bf16[24,36,8,128]{3,2,1,0:T(8,128)(2,1)}, u32[]{:S(2)}) copy-start(bf16[24,36,8,128]{3,2,1,0:T(8,128)(2,1)} %copy-done.21) | copy-start | bytes 5308420
  408.7 17.6 %all-to-all-start.4 = ((bf16[8,16,3072]{2,1,0:T(8,128)(2,1)}), bf16[8,16,3072]{2,1,0:T(8,128)(2,1)S(1)}, u32[]{:S(2)}, u32[]{:S(2)}) async-start(bf16[8,16,3072]{2,1,0:T(8,128)(2,1)} %get-tuple-element.16), calls=%async_computation.4 | async-start | bytes 1572864 | tf_op jit(solution)/shard_map/all_to_all | solution.py:174
  426.3 17.5 %all-to-all-start.3 = ((bf16[8,16,3072]{2,1,0:T(8,128)(2,1)}), bf16[8,16,3072]{2,1,0:T(8,128)(2,1)}, u32[]{:S(2)}, u32[]{:S(2)}) async-start(bf16[8,16,3072]{2,1,0:T(8,128)(2,1)} %get-tuple-element.17), calls=%async_computation.3 | async-start | bytes 1572864 | tf_op jit(solution)/shard_map/all_to_all | solution.py:167
  449.1 41.8 %copy-start.1 = (bf16[288,3072]{1,0:T(8,128)(2,1)S(1)}, bf16[288,3072]{1,0:T(8,128)(2,1)}, u32[]{:S(2)}) copy-start(bf16[288,3072]{1,0:T(8,128)(2,1)} %param.19) | copy-start | bytes 5308420
  (35 other events, 97.4 us)
Sparse Core Ops, SparseCore 0:
  9.7 130.1 all-gather.1
  192.7 213.4 reduce-scatter.4
  409.9 79.2 reduce-scatter.6
where the time goes:
time: 504 us; the launch traced here: 498 us
  waiting for transfers between devices  236 us (47%)
  local copies, waits for them, and re-layouts  85 us (17%)
  matrix products  74 us (15%)
  other arithmetic  52.6 us (10%)
  starting transfers between devices  35.6 us (7%)
  between operations  14.5 us (3%)
    reduce_scatter x1, waiting for transfers between devices, shards(): lax.psum_scatter((lax.dot_general(attn, out_grad, (((0,), (0,)), ((), ())...  165 us
    gather x6, local copies, waits for them, and re-layouts, from_pool(): return jnp.take(pooled, row_source, axis=0)  37.1 us
    unnamed x4, waiting for transfers between devices  35.5 us
    dot_general x3, matrix products, attention(): scores = jnp.einsum('ahd,bhd->hab', query_heads, key_heads) * HD ** (-0.5)  25.6 us
    gather x6, local copies, waits for them, and re-layouts, take_slots(): jnp.take(matrix, slot_source.reshape(-1), axis=0)  19.9 us
    all_to_all x1, waiting for transfers between devices, shards(): lax.all_to_all(take_slots(key_vectors, send_source, send_valid), 'dp', sp...  17.7 us
    all_to_all x1, waiting for transfers between devices, shards(): lax.all_to_all(take_slots(queries, send_source, send_valid), 'dp', split_...  16.2 us
    sub x1, other arithmetic, attention(): powers = jnp.exp(scores - row_max)  15.2 us
  transfers between devices with their start and end apart: 9, of which 6 were waited for; matrix products, arithmetic and copies ran while one was open for 34% of the time, Pallas kernels for 0%

commit v1 on v0

--- a/solution.py
+++ b/solution.py
@@ -87,29 +87,6 @@
         )
         > 0
     )
-    got_q, got_k, got_v = (
-        lax.all_to_all(
-            take_slots(queries, send_source, send_valid),
-            "dp",
-            split_axis=0,
-            concat_axis=0,
-            tiled=True,
-        ),
-        lax.all_to_all(
-            take_slots(key_vectors, send_source, send_valid),
-            "dp",
-            split_axis=0,
-            concat_axis=0,
-            tiled=True,
-        ),
-        lax.all_to_all(
-            take_slots(value_vectors, send_source, send_valid),
-            "dp",
-            split_axis=0,
-            concat_axis=0,
-            tiled=True,
-        ),
-    )
     senders = peers[:, None]
     arriving = grp_dest == dp_index
     source_base = jnp.where(senders == dp_index, grp_start, row_count + senders * SLOT) - grp_off
@@ -121,37 +98,6 @@
     row_source = jnp.sum(
         jnp.where(covers, source_base[:, :, None] + row_ids[None, None, :], 0), axis=(0, 1)
     )
-    image_ids = senders * img_count + jnp.arange(img_count, dtype=jnp.int32)[None, :]
-    segment = jnp.sum(jnp.where(covers, image_ids[:, :, None], 0), axis=(0, 1))
-    moved_q = from_pool(queries, got_q, row_source)
-    moved_k = from_pool(key_vectors, got_k, row_source)
-    moved_v = from_pool(value_vectors, got_v, row_source)
-    same_image = segment[:, None] == segment[None, :]
-    attn, pullback = jax.vjp(
-        lambda first_in, second_in, third_in: attention(first_in, second_in, third_in, same_image),
-        moved_q,
-        moved_k,
-        moved_v,
-    )
-    full_weight = lax.all_gather(out_weight, "fsdp", axis=0, tiled=True)
-    projected = jnp.dot(attn, full_weight, preferred_element_type=jnp.float32)
-    attn_grad = lax.dot_general(
-        out_grad, full_weight, (((1,), (1,)), ((), ())), preferred_element_type=jnp.float32
-    ).astype(jnp.bfloat16)
-    grad_q, grad_k, grad_v = pullback(attn_grad)
-    grad_scale = (row_count * dp_count * fs_count) ** (-0.5)
-    weight_shard = lax.psum_scatter(
-        (
-            lax.dot_general(
-                attn, out_grad, (((0,), (0,)), ((), ())), preferred_element_type=jnp.float32
-            )
-            * grad_scale
-        ).astype(jnp.bfloat16),
-        "fsdp",
-        scatter_dimension=0,
-        tiled=True,
-    )
-    weight_grad = lax.psum_scatter(weight_shard, "dp", scatter_dimension=1, tiled=True)
     returning = arriving & (senders != dp_index)
     back_source = jnp.sum(jnp.where(returning, grp_off, 0), axis=1)[:, None] + slot_ids[None, :]
     back_valid = (
@@ -163,39 +109,49 @@
         )
         > 0
     )
-    home_q, home_k, home_v = (
-        lax.all_to_all(
-            take_slots(grad_q, back_source, back_valid),
-            "dp",
-            split_axis=0,
-            concat_axis=0,
-            tiled=True,
-        ),
-        lax.all_to_all(
-            take_slots(grad_k, back_source, back_valid),
-            "dp",
-            split_axis=0,
-            concat_axis=0,
-            tiled=True,
-        ),
-        lax.all_to_all(
-            take_slots(grad_v, back_source, back_valid),
-            "dp",
-            split_axis=0,
-            concat_axis=0,
-            tiled=True,
-        ),
-    )
     stays = own_dest == dp_index
     home_base = jnp.where(stays, own_off, row_count + own_dest * SLOT) - own_start
     inside = (row_ids[None, :] >= own_start[:, None]) & (
         row_ids[None, :] < (own_start + own_len)[:, None]
     )
     home_source = jnp.sum(jnp.where(inside, home_base[:, None] + row_ids[None, :], 0), axis=0)
-    query_grad = from_pool(grad_q, home_q, home_source)
-    key_grad = from_pool(grad_k, home_k, home_source)
-    value_grad = from_pool(grad_v, home_v, home_source)
-    return (projected.astype(jnp.bfloat16), query_grad, key_grad, value_grad, weight_grad)
+    segment = jnp.sum(jnp.where(row_ids[None, :] >= own_start[:, None], 1, 0), axis=0)
+    home_og = lax.all_to_all(
+        take_slots(out_grad, back_source, back_valid), "dp", split_axis=0, concat_axis=0, tiled=True
+    )
+    grad_rows = from_pool(out_grad, home_og, home_source)
+    same_image = segment[:, None] == segment[None, :]
+    attn, pullback = jax.vjp(
+        lambda first_in, second_in, third_in: attention(first_in, second_in, third_in, same_image),
+        queries,
+        key_vectors,
+        value_vectors,
+    )
+    full_weight = lax.all_gather(out_weight, "fsdp", axis=0, tiled=True)
+    projected = jnp.dot(attn, full_weight, preferred_element_type=jnp.float32)
+    attn_grad = lax.dot_general(
+        grad_rows, full_weight, (((1,), (1,)), ((), ())), preferred_element_type=jnp.float32
+    ).astype(jnp.bfloat16)
+    grad_q, grad_k, grad_v = pullback(attn_grad)
+    grad_scale = (row_count * dp_count * fs_count) ** (-0.5)
+    weight_shard = lax.psum_scatter(
+        (
+            lax.dot_general(
+                attn, grad_rows, (((0,), (0,)), ((), ())), preferred_element_type=jnp.float32
+            )
+            * grad_scale
+        ).astype(jnp.bfloat16),
+        "fsdp",
+        scatter_dimension=0,
+        tiled=True,
+    )
+    weight_grad = lax.psum_scatter(weight_shard, "dp", scatter_dimension=1, tiled=True)
+    projected = projected.astype(jnp.bfloat16)
+    got_rows = lax.all_to_all(
+        take_slots(projected, send_source, send_valid), "dp", split_axis=0, concat_axis=0, tiled=True
+    )
+    projected = from_pool(projected, got_rows, row_source)
+    return (projected, grad_q, grad_k, grad_v, weight_grad)
 
 
 def solution(mesh):

time: 504 us -> 464 us (0.921)
  waiting for transfers between devices: 236 us -> 280 us
  local copies, waits for them, and re-layouts: 85 us -> 42.1 us
  other arithmetic: 52.6 us -> 29.1 us
  starting transfers between devices: 35.6 us -> 14.7 us
    all_gather x1, waiting for transfers between devices: 0.01 us -> 57.8 us  [shards(): full_weight = lax.all_gather(out_weight, 'fsdp', axis=0, tiled=True)]
    all_to_all x6 -> x2, waiting for transfers between devices: 35.4 us -> 0.01 us  [the longest x1 0.01 us: shards(): lax.all_to_all(take_slots(out_grad, back_source, back_valid), 'dp', split...]
    all_to_all x6 -> x2, starting transfers between devices: 35.3 us -> 14.6 us  [the longest x1 8.32 us: shards(): lax.all_to_all(take_slots(out_grad, back_source, back_valid), 'dp', split...]
    gather x6 -> x2, local copies, waits for them, and re-layouts: 37.1 us -> 17 us  [from_pool(): return jnp.take(pooled, row_source, axis=0)]
    gather x6 -> x2, local copies, waits for them, and re-layouts: 19.9 us -> 4.58 us  [take_slots(): jnp.take(matrix, slot_source.reshape(-1), axis=0)]
    reduce_scatter x1, waiting for transfers between devices: 165 us -> 179 us  [shards(): lax.psum_scatter((lax.dot_general(attn, grad_rows, (((0,), (0,)), ((), ()...]
    concatenate x6 -> x2, other arithmetic: 13.6 us -> 4.4 us  [from_pool(): jnp.concatenate([local_rows, arrived.reshape(arrived.shape[0] * arrived.s...]
    unnamed x4, waiting for transfers between devices: 35.5 us -> 42.8 us
  transfers between devices with their start and end apart: 9 -> 5, of which waited for: 6 -> 3; matrix products, arithmetic and copies ran while one was open for 34% -> 23% of each run, Pallas kernels for 0% -> 0%
where the time goes in v1:
time: 464 us; the launch traced here: 456 us
  waiting for transfers between devices  280 us (60%)
  matrix products  75.7 us (16%)
  local copies, waits for them, and re-layouts  42.1 us (9%)
  other arithmetic  29.1 us (6%)
  starting transfers between devices  14.7 us (3%)
  between operations  14.5 us (3%)
    reduce_scatter x1, waiting for transfers between devices, shards(): lax.psum_scatter((lax.dot_general(attn, grad_rows, (((0,), (0,)), ((), ()...  179 us
    all_gather x1, waiting for transfers between devices, shards(): full_weight = lax.all_gather(out_weight, 'fsdp', axis=0, tiled=True)  57.8 us
    unnamed x4, waiting for transfers between devices  42.8 us
    dot_general x3, matrix products, attention(): scores = jnp.einsum('ahd,bhd->hab', query_heads, key_heads) * HD ** (-0.5)  28.1 us
    gather x2, local copies, waits for them, and re-layouts, from_pool(): return jnp.take(pooled, row_source, axis=0)  17 us
    sub x1, other arithmetic, attention(): powers = jnp.exp(scores - row_max)  15.4 us
    dot_general x3, matrix products, attention(): mixed = jnp.einsum('hab,bhd->ahd', weights.astype(jnp.float32), value_heads)  14.7 us
    dot_general x1, matrix products, shards(): lax.dot_general(attn, grad_rows, (((0,), (0,)), ((), ())), preferred_elem...  13.4 us
  transfers between devices with their start and end apart: 5, of which 3 were waited for; matrix products, arithmetic and copies ran while one was open for 23% of the time, Pallas kernels for 0%

profile of v1, /device:TPU:1, one launch (start us, length us, event | category | flops | bytes accessed | tf_op | source)
XLA Modules:
  0.0 456.1 jit_solution(17761645140288929949)
XLA Ops:
  13.5 3.5 gather_fusion.2
  18.3 8.3 %all-to-all-start.1 = ((bf16[8,16,3072]{2,1,0:T(8,128)(2,1)}), bf16[8,16,3072]{2,1,0:T(8,128)(2,1)}, u32[]{:S(2)}, u32[]{:S(2)}) async-start(bf16[8,16,3072]{2,1,0:T(8,128)(2,1)} %broadcast_select_fusion.4), calls=%async_computation.1 | async-start | bytes 1572864 | tf_op jit(solution)/shard_map/all_to_all | solution.py:119
  29.5 7.0 %fusion.19 = f32[24,288,288]{1,2,0:T(8,128)} fusion(bf16[288,3072]{1,0:T(8,128)(2,1)} %param.13, bf16[288,3072]{1,0:T(8,128)(2,1)S(1)} %copy-done.4), kind=kOutput, calls=%fused_computation.38 | convolution fusion | flops 509607936 | bytes 11501568 | tf_op jit(solution)/shard_map/jvp(ahd,bhd->hab)/dot_general | solution.py:16
  36.5 15.4 %fusion.56 = (f32[24,288]{1,0:T(8,128)S(1)}, f32[24,288,288]{1,2,0:T(8,128)}) fusion(f32[24,288,288]{1,2,0:T(8,128)} %fusion.19, pred[288,288]{0,1:T(8,128)(4,1)S(1)} %broadcast_compare_fusion), kind=kOutput, calls=%fused_computation.125 | output fusion | flops 11944223 | bytes 16035840 | tf_op jit(solution)/shard_map/jvp()/sub | solution.py:19
  53.8 2.7 pad_maximum_fusion.1
  56.5 8.7 %gather_fusion.3 = bf16[288,3072]{1,0:T(8,128)(2,1)S(1)} fusion(bf16[416,3072]{1,0:T(8,128)(2,1)} %pad_maximum_fusion.1, s32[1024]{0:T(1024)} %pad_clamp_fusion), kind=kCustom, calls=%fused_computation.3.clone | custom fusion | bytes 3540096 | tf_op jit(solution)/shard_map/jit(_take)/gather | solution.py:40
  65.3 57.8 %all-gather.2.cloned.1.call-done = bf16[3072,3072]{1,0:T(8,128)(2,1)} async-done(((bf16[192,3072]{1,0:T(8,128)(2,1)}), bf16[3072,3072]{1,0:T(8,128)(2,1)}) %all-gather.2.cloned.1.call-update) | async-done | bytes 18874384 | tf_op jit(solution)/shard_map/all_gather | solution.py:130
  123.1 9.9 %fusion.40 = bf16[36,24,8,128]{3,2,1,0:T(8,128)(2,1)S(1)} fusion(bf16[3072,3072]{1,0:T(8,128)(2,1)} %all-gather.2.cloned.1.call-done, bf16[288,3072]{1,0:T(8,128)(2,1)S(1)} %gather_fusion.3, pred[288]{0:T(512)(128)(4,1)} %compare_and_fusion), kind=kOutput, calls=%fused_computation.59 | convolution fusion | flops 5437587456 | bytes 22413600 | tf_op jit(solution)/shard_map/dot_general | solution.py:132
  133.0 8.1 %fusion.6 = (f32[24,288]{1,0:T(8,128)}, bf16[24,288,288]{1,2,0:T(8,128)(2,1)S(1)}, bf16[24,288,288]{1,2,0:T(8,128)(2,1)}) fusion(f32[24,288,288]{1,2,0:T(8,128)} %get-tuple-element.18, f32[24,288]{1,0:T(8,128)S(1)} %copy-done.22, f32[24,288]{1,0:T(8,128)S(1)} %copy-done.18, bf16[36,24,8,128]{3,2,1,0:T(8,128)(2,1)S(1)} %fusion.40, ...), kind=kOutput, calls=%fused_computation.13 | convolution fusion | flops 523535616 | bytes 19547136 | tf_op jit(solution)/shard_map/transpose(jvp(hab,bhd->ahd))/dot_general | solution.py:21
  141.1 2.3 copy-done.3
  143.4 1.9 convert_bitcast_fusion.3
  146.6 13.4 %multiply_convert_fusion = bf16[3072,3072]{1,0:T(8,128)(2,1)} fusion(bf16[24,36,8,128]{3,2,1,0:T(8,128)(2,1)S(1)} %convert_bitcast_fusion.3, bf16[288,3072]{1,0:T(8,128)(2,1)S(1)} %gather_fusion.3, pred[288]{0:T(512)(128)(4,1)S(1)} %copy-done.30), kind=kOutput, calls=%fused_computation.5 | convolution fusion | flops 5455577088 | bytes 22413600 | tf_op jit(solution)/shard_map/dot_general | solution.py:139
  163.0 9.8 %convolution_convert_fusion.1 = bf16[288,3072]{1,0:T(8,128)(2,1)S(1)} fusion(bf16[3072,3072]{1,0:T(8,128)(2,1)} %all-gather.2.cloned.1.call-done, bf16[24,36,8,128]{3,2,1,0:T(8,128)(2,1)S(1)} %copy-done.8), kind=kOutput, calls=%fused_computation.22 | convolution fusion | flops 5436702720 | bytes 22413312 | tf_op jit(solution)/shard_map/dot_general | solution.py:131
  175.0 6.3 %all-to-all-start = ((bf16[8,16,3072]{2,1,0:T(8,128)(2,1)}), bf16[8,16,3072]{2,1,0:T(8,128)(2,1)S(1)}, u32[]{:S(2)}, u32[]{:S(2)}) async-start(bf16[8,16,3072]{2,1,0:T(8,128)(2,1)} %broadcast_select_fusion.5), calls=%async_computation | async-start | bytes 1572864 | tf_op jit(solution)/shard_map/all_to_all | solution.py:150
  181.3 10.4 %convert_bitcast_fusion.1 = bf16[24,36,8,128]{3,2,1,0:T(8,128)(2,1)} fusion(f32[24,288,288]{1,2,0:T(8,128)} %get-tuple-element.18, bf16[24,288,288]{1,2,0:T(8,128)(2,1)} %get-tuple-element.19, f32[24,288]{1,0:T(8,128)S(1)} %copy-done.21, f32[24,288]{1,0:T(8,128)S(1)} %copy-done.19, pred[288,288]{0,1:T(8,128)(4,1)S(1)} %copy-done.16, ...), kind=kOutput, calls=%fused_computation.44 | convolution fusion | flops 522436608 | bytes 15621120 | tf_op jit(solution)/shard_map/transpose(jvp(ahd,bhd->hab))/dot_general | solution.py:16
  191.7 179.2 %reduce-scatter.5.cloned.1.call-done = bf16[192,3072]{1,0:T(8,128)(2,1)} async-done(((bf16[3072,3072]{1,0:T(8,128)(2,1)}), bf16[192,3072]{1,0:T(8,128)(2,1)}) %reduce-scatter.5.cloned.1.call-update) | async-done | bytes 1179664 | tf_op jit(solution)/shard_map/reduce_scatter | solution.py:137
  371.0 2.7 copy.102
  373.7 10.7 %convert_bitcast_fusion.2 = bf16[24,36,8,128]{3,2,1,0:T(8,128)(2,1)} fusion(f32[24,288,288]{1,2,0:T(8,128)} %get-tuple-element.18, bf16[24,288,288]{1,2,0:T(8,128)(2,1)} %get-tuple-element.19, f32[24,288]{1,0:T(8,128)S(1)} %copy-done.21, f32[24,288]{1,0:T(8,128)S(1)} %copy-done.19, pred[288,288]{0,1:T(8,128)(4,1)S(1)} %copy-done.16, ...), kind=kOutput, calls=%fused_computation.45 | convolution fusion | flops 522436608 | bytes 15621120 | tf_op jit(solution)/shard_map/transpose(jvp(ahd,bhd->hab))/dot_general | solution.py:16
  384.4 4.6 %convert_bitcast_fusion = bf16[24,36,8,128]{3,2,1,0:T(8,128)(2,1)S(1)} fusion(bf16[24,288,288]{1,2,0:T(8,128)(2,1)} %copy-done.3, bf16[36,24,8,128]{3,2,1,0:T(8,128)(2,1)} %copy-done.31), kind=kOutput, calls=%fused_computation.43 | convolution fusion | flops 510492672 | bytes 7520256 | tf_op jit(solution)/shard_map/transpose(jvp(hab,bhd->ahd))/dot_general | solution.py:21
  389.0 1.7 copy.159
  390.7 1.7 copy.161
  395.8 8.3 %gather_fusion.1 = bf16[288,3072]{1,0:T(8,128)(2,1)S(1)} fusion(bf16[416,3072]{1,0:T(8,128)(2,1)} %pad_maximum_fusion, s32[1024]{0:T(1024)S(1)} %pad_clamp_fusion.2), kind=kCustom, calls=%fused_computation.1.clone | custom fusion | bytes 3540096 | tf_op jit(solution)/shard_map/jit(_take)/gather | solution.py:40
  405.5 42.1 %reduce-scatter.7.cloned.1.call-done = bf16[384,192]{1,0:T(8,128)(2,1)} async-done(((bf16[3072,192]{1,0:T(8,128)(2,1)}), bf16[384,192]{1,0:T(8,128)(2,1)}) %reduce-scatter.7.cloned.1.call-update) | async-done | bytes 147472
  447.6 1.7 copy.103
  (134 shorter events, 23.3 us)
Async XLA Ops:
  7.2 125.8 %copy-start = (bf16[288,3072]{1,0:T(8,128)(2,1)S(1)}, bf16[288,3072]{1,0:T(8,128)(2,1)}, u32[]{:S(2)}) copy-start(bf16[288,3072]{1,0:T(8,128)(2,1)} %param.14) | copy-start | bytes 5308420
  7.2 115.9 %all-gather.2.cloned.1.call-start = ((), (), s32[]{:S(2)}) async-start(), calls=%async_computation.4 | async-start | bytes 20054016 | tf_op jit(solution)/shard_map/all_gather | solution.py:130
  8.7 4.8 %copy-start.11 = (s32[8,16,6]{1,0,2:T(8,128)}, s32[8,16,6]{1,0,2:T(8,128)S(1)}, u32[]{:S(2)}) copy-start(s32[8,16,6]{1,0,2:T(8,128)S(1)} %reshape.327) | copy-start | bytes 9220
  10.2 3.3 copy-start.12
  17.3 12.2 %copy-start.4 = (bf16[288,3072]{1,0:T(8,128)(2,1)S(1)}, bf16[288,3072]{1,0:T(8,128)(2,1)}, u32[]{:S(2)}) copy-start(bf16[288,3072]{1,0:T(8,128)(2,1)} %param.12) | copy-start | bytes 5308420
  18.3 35.4 %all-to-all-start.1 = ((bf16[8,16,3072]{2,1,0:T(8,128)(2,1)}), bf16[8,16,3072]{2,1,0:T(8,128)(2,1)}, u32[]{:S(2)}, u32[]{:S(2)}) async-start(bf16[8,16,3072]{2,1,0:T(8,128)(2,1)} %broadcast_select_fusion.4), calls=%async_computation.1 | async-start | bytes 1572864 | tf_op jit(solution)/shard_map/all_to_all | solution.py:119
  26.7 344.3 %reduce-scatter.5.cloned.1.call-start = ((), (), s32[]{:S(2)}) async-start(), calls=%async_computation.5 | async-start | bytes 20054016 | tf_op jit(solution)/shard_map/reduce_scatter | solution.py:137
  29.5 7.0 %copy-start.15 = (pred[288,288]{0,1:T(8,128)(4,1)}, pred[288,288]{0,1:T(8,128)(4,1)S(1)}, u32[]{:S(2)}) copy-start(pred[288,288]{0,1:T(8,128)(4,1)S(1)} %broadcast_compare_fusion) | copy-start | bytes 248836
  36.5 17.3 %copy-start.2 = (bf16[288,3072]{1,0:T(8,128)(2,1)S(1)}, bf16[288,3072]{1,0:T(8,128)(2,1)}, u32[]{:S(2)}) copy-start(bf16[288,3072]{1,0:T(8,128)(2,1)} %param.19) | copy-start | bytes 5308420
  123.1 9.9 %copy-start.18 = (f32[24,288]{1,0:T(8,128)S(1)}, f32[24,288]{1,0:T(8,128)}, u32[]{:S(2)}) copy-start(f32[24,288]{1,0:T(8,128)} %copy-done.17) | copy-start | bytes 82948
  123.1 9.9 %copy-start.22 = (f32[24,288]{1,0:T(8,128)S(1)}, f32[24,288]{1,0:T(8,128)}, u32[]{:S(2)}) copy-start(f32[24,288]{1,0:T(8,128)} %multiply_divide_fusion) | copy-start | bytes 82948
  133.0 8.1 %copy-start.31 = (bf16[36,24,8,128]{3,2,1,0:T(8,128)(2,1)}, bf16[36,24,8,128]{3,2,1,0:T(8,128)(2,1)S(1)}, u32[]{:S(2)}) copy-start(bf16[36,24,8,128]{3,2,1,0:T(8,128)(2,1)S(1)} %fusion.40) | copy-start | bytes 5308420
  141.1 2.3 copy-start.3
  143.4 3.2 copy-start.30
  160.0 2.3 copy-start.20
  160.0 2.9 copy-start.8
  173.8 7.5 %copy-start.16 = (pred[288,288]{0,1:T(8,128)(4,1)S(1)}, pred[288,288]{0,1:T(8,128)(4,1)}, u32[]{:S(2)}) copy-start(pred[288,288]{0,1:T(8,128)(4,1)} %copy-done.15) | copy-start | bytes 248836
  173.8 7.5 %copy-start.19 = (f32[24,288]{1,0:T(8,128)S(1)}, f32[24,288]{1,0:T(8,128)}, u32[]{:S(2)}) copy-start(f32[24,288]{1,0:T(8,128)} %copy-done.17) | copy-start | bytes 82948
  173.8 7.5 %copy-start.21 = (f32[24,288]{1,0:T(8,128)S(1)}, f32[24,288]{1,0:T(8,128)}, u32[]{:S(2)}) copy-start(f32[24,288]{1,0:T(8,128)} %neg.6) | copy-start | bytes 82948
  175.0 219.1 %all-to-all-start = ((bf16[8,16,3072]{2,1,0:T(8,128)(2,1)}), bf16[8,16,3072]{2,1,0:T(8,128)(2,1)S(1)}, u32[]{:S(2)}, u32[]{:S(2)}) async-start(bf16[8,16,3072]{2,1,0:T(8,128)(2,1)} %broadcast_select_fusion.5), calls=%async_computation | async-start | bytes 1572864 | tf_op jit(solution)/shard_map/all_to_all | solution.py:150
  181.2 266.4 %reduce-scatter.7.cloned.1.call-start = ((), (), s32[]{:S(2)}) async-start(), calls=%async_computation.6 | async-start | bytes 1769472
  389.0 1.7 copy-start.6
  390.7 1.7 copy-start.5
  395.8 53.6 %copy-start.1 = (bf16[288,3072]{1,0:T(8,128)(2,1)S(1)}, bf16[288,3072]{1,0:T(8,128)(2,1)}, u32[]{:S(2)}) copy-start(bf16[288,3072]{1,0:T(8,128)(2,1)} %param.14) | copy-start | bytes 5308420
  (13 other events, 13.0 us)
Sparse Core Ops, SparseCore 0:
  9.7 113.3 all-gather.1
  160.2 210.7 reduce-scatter.4
  374.6 72.9 reduce-scatter.6

commit v2 on v1

v2 whole, which is shorter than its diff:
```python
import jax
import jax.numpy as jnp
from jax import lax
from jax.experimental import pallas as pl
from jax.experimental.pallas import tpu as pltpu
from jax.sharding import PartitionSpec as P

HD = 128
SLOT = 16
MESH = pl.DeviceIdType.MESH
F32 = jnp.float32
BF16 = jnp.bfloat16
ROWS = 288
D = 3072
GROUP = 768
HALF = 384
SHARD = 192
CHUNK = 48
BLOCK = 384
Z_ROWS, X_ROWS, Y_ROWS = 96, 48, 48
SCALE = HD ** (-0.5)


def flip(index, by):
    high = lax.rem(lax.div(index, 2) + by // 2, 2)
    return high * 2 + lax.rem(lax.rem(index, 2) + by % 2, 2)


def contract(first, second, first_dim, second_dim):
    return lax.dot_general(
        first, second, (((first_dim,), (second_dim,)), ((), ())), preferred_element_type=F32
    )


def kernel(
    table,
    images,
    q_hbm,
    k_hbm,
    v_hbm,
    w_hbm,
    og_hbm,
    proj_hbm,
    dq_hbm,
    dk_hbm,
    dv_hbm,
    dw_hbm,
    qv,
    kv,
    vv,
    weight,
    pool,
    og_slots,
    slot_out,
    og_pair,
    attn_half,
    attn_out,
    attn_t,
    probs,
    bias,
    heads6,
    grad_half,
    grad_out,
    grad_in,
    part,
    part_out,
    part_in,
    proj_slots,
    term_z,
    term_x,
    term_y,
    got1_z,
    got1_x,
    got1_y,
    got2_z,
    got2_x,
    got2_y,
    got3_z,
    got3_x,
    got3_y,
    dw_rows,
    load_sem,
    store_sem,
    wy_send,
    wy_recv,
    wx_send,
    wx_recv,
    a2a_send,
    a2a_recv,
    core_send,
    core_recv,
    rs_send,
    rs_recv,
):
    dp = lax.axis_index("dp")
    fs = lax.axis_index("fsdp")
    xh, z = lax.div(dp, 4), lax.rem(dp, 4)
    y, xl, core = lax.div(fs, 4), lax.rem(lax.div(fs, 2), 2), lax.rem(fs, 2)

    def device(xh_, xl_, y_, z_, core_):
        return (xh_ * 4 + z_, y_ * 4 + xl_ * 2 + core_)

    def along_x(by):
        return device(lax.rem(xh + by // 2, 2), lax.rem(xl + by % 2, 2), y, z, core)

    def along_y(by):
        return device(xh, xl, flip(y, by), z, core)

    def along_z(by):
        return device(xh, xl, y, flip(z, by), core)

    def over_dp(by):
        return device(lax.rem(xh + by // 4, 2), xl, y, flip(z, by % 4), core)

    partner = device(xh, xl, y, z, 1 - core)

    def remote(src, dst, send, recv, target):
        return pltpu.make_async_remote_copy(
            src_ref=src, dst_ref=dst, send_sem=send, recv_sem=recv, device_id=target, device_id_type=MESH
        )

    here = y * 2 + xl
    loads = [
        pltpu.make_async_copy(
            w_hbm, weight.at[pl.ds(pl.multiple_of(here * SHARD, SHARD), SHARD)], load_sem.at[0]
        ),
        pltpu.make_async_copy(og_hbm, pool.at[0:ROWS], load_sem.at[1]),
        pltpu.make_async_copy(q_hbm, qv, load_sem.at[2]),
        pltpu.make_async_copy(k_hbm, kv, load_sem.at[3]),
        pltpu.make_async_copy(v_hbm, vv, load_sem.at[4]),
    ]
    for copy in loads:
        copy.start()
    barrier = pltpu.get_barrier_semaphore()
    peers = (
        [along_x(by) for by in (1, 2, 3)]
        + [along_y(by) for by in (1, 2, 3)]
        + [along_z(by) for by in (1, 2, 3)]
        + [over_dp(by) for by in (5, 6, 7)]
        + [partner]
    )
    for peer in peers:
        pl.semaphore_signal(barrier, inc=1, device_id=peer, device_id_type=MESH)

    bias[...] = jnp.where(table[:, 2:3] == images[...], 0.0, -1e30).astype(F32)

    def pick(column, out_rows, in_rows, dst, dst_core=None):
        chosen = lax.broadcasted_iota(jnp.int32, (out_rows, in_rows), 1) == (
            table[:out_rows, column : column + 1]
        )
        one_hot = jnp.where(chosen, 1.0, 0.0).astype(BF16)

        def one_part(i, carry):
            cols = pl.ds(pl.multiple_of(i * GROUP, GROUP), GROUP)
            rows = contract(one_hot, pool[:in_rows, cols], 1, 0).astype(BF16)
            if dst_core is None:
                dst[:, cols] = rows
            else:
                dst[dst_core, :, cols] = rows
            return carry

        lax.fori_loop(0, D // GROUP, one_part, 0)

    pl.semaphore_wait(barrier, len(peers))

    def shard_rows(y_, xl_, chunk):
        return pl.ds(pl.multiple_of((y_ * 2 + xl_) * SHARD + chunk * CHUNK, CHUNK), CHUNK)

    def w_along_y(by, chunk):
        rows = weight.at[shard_rows(y, xl, chunk)]
        return remote(
            rows, rows, wy_send.at[by - 1, chunk], wy_recv.at[by - 1, chunk], along_y(by)
        )

    def w_along_x(by, chunk):
        rows = weight.at[shard_rows(flip(y, by), xl, chunk)]
        return remote(
            rows, rows, wx_send.at[by, chunk], wx_recv.at[by, chunk], along_x(1 if chunk < 2 else 3)
        )

    def forward(by, chunk):
        w_along_y(by, chunk).wait_recv()
        w_along_x(by, chunk).start()

    loads[0].wait()
    for step in range(4):
        w_along_y(1, (0, 2, 1, 3)[step]).start()
        w_along_y(3, (2, 0, 3, 1)[step]).start()
        w_along_x(0, (0, 2, 1, 3)[step]).start()

    def unit(index):
        return pl.ds(pl.multiple_of(index * SLOT, SLOT), SLOT)

    def slots(by, dst, phase):
        to_dp = lax.rem(xh + by // 4, 2) * 4 + flip(z, by % 4)
        return remote(
            slot_out.at[unit(to_dp)],
            dst.at[unit(dp)],
            a2a_send.at[phase, by - 1],
            a2a_recv.at[phase, by - 1],
            over_dp(by),
        )

    loads[1].wait()
    pick(3, 8 * SLOT, ROWS, slot_out)
    own_slot = jnp.zeros((SLOT, D), BF16)
    og_slots[unit(dp), :] = own_slot
    proj_slots[unit(dp), :] = own_slot
    for by in range(1, 8):
        slots(by, og_slots, 0).start()
    for copy in loads[2:]:
        copy.wait()

    def head_cols(head):
        return pl.ds(pl.multiple_of(head * HD, HD), HD)

    def split_cores(first, second):
        mine = jnp.where(core == 0, first, second)
        other = jnp.where(core == 0, second, first)
        return mine, other

    def attn_copy(group):
        return remote(
            attn_out.at[group],
            attn_half.at[core, group],
            core_send.at[0, group],
            core_recv.at[0, group],
            partner,
        )

    def attend(group):
        def one_head(i, carry):
            head = group * 6 + i
            cols = head_cols(head)
            scores = contract(qv[:, cols], kv[:, cols], 1, 1) * SCALE + bias[...]
            powers = jnp.exp(scores - jnp.max(scores, axis=1, keepdims=True))
            inverse = 1.0 / jnp.sum(powers, axis=1, keepdims=True)
            weights = (powers * inverse).astype(BF16)
            probs[head] = weights
            heads6[:, head_cols(i)] = contract(weights, vv[:, cols], 1, 0).astype(BF16)
            return carry

        lax.fori_loop(0, 6, one_head, 0)
        for t in range(2):
            first = heads6[:, t * HALF : t * HALF + SHARD]
            second = heads6[:, t * HALF + SHARD : (t + 1) * HALF]
            mine, other = split_cores(first, second)
            attn_half[core, group, :, t * SHARD : (t + 1) * SHARD] = mine
            attn_out[group, :, t * SHARD : (t + 1) * SHARD] = other
        attn_copy(group).start()

    attend(0)
    attend(1)
    forward(1, 0)
    forward(3, 2)
    attend(2)

    for by in range(1, 8):
        slots(by, og_slots, 0).wait_recv()
    pool[ROWS:, :] = og_slots[...]
    pick(0, ROWS, ROWS + 8 * SLOT, og_pair, core)
    og_copy = remote(
        og_pair.at[core], og_pair.at[core], core_send.at[1, 0], core_recv.at[1, 0], partner
    )
    og_copy.start()
    attend(3)
    forward(1, 2)
    forward(3, 0)
    w_along_y(2, 0).start()
    w_along_y(2, 2).start()

    for group in range(4):
        attn_copy(group).wait_recv()
        attn_t[group] = attn_half[:, group].reshape(2 * ROWS, HALF).T
    og_copy.wait_recv()

    grad_scale = (ROWS * 128) ** (-0.5)

    def copy1_z(xh_, z_, by):
        return remote(
            term_z.at[xh_, z_], got1_z.at[by - 1, xh_], rs_send.at[0, by - 1], rs_recv.at[0, by - 1],
            device(xh, xl, y, z_, core),
        )

    def copy1_x(xh_, xl_, z_, by):
        return remote(
            term_x.at[xh_, xl_, :, z_], got1_x.at[by - 1, :, z_], rs_send.at[1, by - 1],
            rs_recv.at[1, by - 1], device(xh_, xl_, y, z, core),
        )

    def copy1_y(xh_, y_, z_, by):
        return remote(
            term_y.at[y_, z_, xh_], got1_y.at[by - 1, z_, xh_], rs_send.at[2, by - 1],
            rs_recv.at[2, by - 1], device(xh, xl, y_, z, core),
        )

    def one_term(i, carry):
        by_z, by_xh = 3 - lax.div(i, 2), 1 - lax.rem(i, 2)
        z_ = lax.rem(lax.div(z, 2) + lax.div(by_z, 2), 2) * 2 + lax.rem(z + by_z, 2)
        xh_ = lax.rem(xh + by_xh, 2)
        cols = pl.ds(pl.multiple_of((xh_ * 4 + z_) * BLOCK, BLOCK), BLOCK)
        grads = og_pair[:, :, cols].reshape(2 * ROWS, BLOCK)
        for group in range(4):
            term = (contract(attn_t[group], grads, 1, 0) * grad_scale).astype(BF16)
            for xl_ in range(2):
                at = xl_ * SHARD
                term_z[xh_, z_, xl_, group] = term[at : at + Z_ROWS]
                term_x[xh_, xl_, group, z_] = term[at + Z_ROWS : at + Z_ROWS + X_ROWS]
                term_y[group, z_, xh_, xl_] = term[at + Z_ROWS + X_ROWS : at + SHARD]

        @pl.when(by_z > 0)
        def _():
            copy1_z(xh_, z_, by_z).start()

        for by_xl in range(2):

            @pl.when(by_xh * 2 + by_xl > 0)
            def _():
                copy1_x(xh_, lax.rem(xl + by_xl, 2), z_, by_xh * 2 + by_xl).start()

        for by_y in (1, 2, 3):
            copy1_y(xh_, flip(y, by_y), z_, by_y).start()
        return carry

    lax.fori_loop(0, 4, one_term, 0)
    forward(1, 1)
    forward(3, 3)
    w_along_y(2, 1).start()
    w_along_y(2, 3).start()
    lax.fori_loop(4, 8, one_term, 0)
    forward(1, 3)
    forward(3, 1)

    def grad_copy(by):
        return remote(
            grad_out.at[by], grad_in.at[by], core_send.at[2, by], core_recv.at[2, by], partner
        )

    def attn_grad(by):
        for chunk in range(4):
            w_along_x(by, chunk).wait_recv()
        rows = pl.ds(pl.multiple_of(flip(y, by) * HALF, HALF), HALF)

        def one_side(side, carry):
            owner = lax.rem(1 - core + side, 2)
            half = contract(og_pair[owner], weight[rows, :], 1, 1).astype(BF16)

            @pl.when(side == 0)
            def _():
                grad_out[by] = half

            @pl.when(side == 1)
            def _():
                grad_half[by] = half

            return carry

        one_side(0, 0)
        grad_copy(by).start()
        one_side(1, 0)

    def store_copy(by, which):
        cols = pl.ds(pl.multiple_of(flip(y, by) * GROUP, GROUP), GROUP)
        src = (qv, kv, vv)[which]
        dst = (dq_hbm, dk_hbm, dv_hbm)[which]
        return pltpu.make_async_copy(src.at[:, cols], dst.at[:, cols], store_sem.at[which, by])

    def attend_back(by):
        grad_copy(by).wait_recv()
        for t in range(2):
            mine = grad_half[by, :, t * SHARD : (t + 1) * SHARD]
            other = grad_in[by, :, t * SHARD : (t + 1) * SHARD]
            first, second = split_cores(mine, other)
            heads6[:, t * HALF : t * HALF + SHARD] = first
            heads6[:, t * HALF + SHARD : (t + 1) * HALF] = second

        def one_head(i, carry):
            head = flip(y, by) * 6 + i
            cols = head_cols(head)
            grads = heads6[:, head_cols(i)]
            weights = probs[head]
            wide = weights.astype(F32)
            queries, keys = qv[:, cols], kv[:, cols]
            products = contract(grads, vv[:, cols], 1, 1) * wide
            total = jnp.sum(products, axis=1, keepdims=True)
            score_grad = ((products - wide * total) * SCALE).astype(BF16)
            vv[:, cols] = contract(weights, grads, 0, 0).astype(BF16)
            qv[:, cols] = contract(score_grad, keys, 1, 0).astype(BF16)
            kv[:, cols] = contract(score_grad, queries, 0, 0).astype(BF16)
            return carry

        lax.fori_loop(0, 6, one_head, 0)
        for which in range(3):
            store_copy(by, which).start()

    attn_grad(0)
    attend_back(0)
    forward(2, 0)
    forward(2, 2)
    attn_grad(1)
    attend_back(1)
    forward(2, 1)
    attn_grad(3)
    forward(2, 3)
    attend_back(3)
    attn_grad(2)

    def part_copy(block):
        return remote(
            part_out.at[block], part_in.at[block], core_send.at[3, block], core_recv.at[3, block],
            partner,
        )

    def one_block(block, carry):
        cols = pl.ds(pl.multiple_of(block * BLOCK, BLOCK), BLOCK)
        total = jnp.zeros((2 * ROWS, BLOCK), F32)
        for group in range(4):
            total += contract(
                attn_half[:, group].reshape(2 * ROWS, HALF),
                weight[group * HALF : (group + 1) * HALF, cols],
                1,
                0,
            )
        part[...] = total.reshape(2, ROWS, BLOCK)
        part_out[block] = part[1 - core].astype(BF16)
        part_copy(block).start()
        pool[:ROWS, cols] = part[core].astype(BF16)
        return carry

    lax.fori_loop(0, 8, one_block, 0)

    def add_block(block, carry):
        cols = pl.ds(pl.multiple_of(block * BLOCK, BLOCK), BLOCK)
        part_copy(block).wait_recv()
        pool[:ROWS, cols] = (
            pool[:ROWS, cols].astype(F32) + part_in[block].astype(F32)
        ).astype(BF16)
        return carry

    lax.fori_loop(0, 8, add_block, 0)

    for by in range(1, 8):
        slots(by, og_slots, 0).wait_send()
    pick(4, 8 * SLOT, ROWS, slot_out)
    for by in range(1, 8):
        slots(by, proj_slots, 1).start()

    attend_back(2)

    def all_of(buffer, sem):
        return pltpu.make_async_copy(buffer, buffer, sem)

    def summed(own, others):
        total = own.astype(F32)
        for other in others:
            total += other.astype(F32)
        return total

    def wait_got(buffer, kind):
        for by in (1, 2, 3):
            all_of(buffer.at[by - 1], rs_recv.at[kind, by - 1]).wait()

    wait_got(got1_z, 0)

    def sum1_z(i, carry):
        xh_, xl_, y_ = lax.div(i, 8), lax.rem(lax.div(i, 4), 2), lax.rem(i, 4)
        term_z[xh_, z, xl_, y_] = summed(
            term_z[xh_, z, xl_, y_], [got1_z[r, xh_, xl_, y_] for r in range(3)]
        ).astype(BF16)
        return carry

    lax.fori_loop(0, 16, sum1_z, 0)

    def copy2_z(by):
        xh_, xl_ = lax.rem(xh + by // 2, 2), lax.rem(xl + by % 2, 2)
        return remote(
            term_z.at[xh_, z, xl_], got2_z.at[by - 1], rs_send.at[3, by - 1], rs_recv.at[3, by - 1],
            along_x(by),
        )

    for by in (1, 2, 3):
        copy2_z(by).start()

    wait_got(got1_x, 1)

    def sum1_x(i, carry):
        y_, z_ = lax.div(i, 4), lax.rem(i, 4)
        term_x[xh, xl, y_, z_] = summed(
            term_x[xh, xl, y_, z_], [got1_x[r, y_, z_] for r in range(3)]
        ).astype(BF16)
        return carry

    lax.fori_loop(0, 16, sum1_x, 0)

    def copy2_x(by):
        return remote(
            term_x.at[xh, xl, flip(y, by)], got2_x.at[by - 1], rs_send.at[4, by - 1],
            rs_recv.at[4, by - 1], along_y(by),
        )

    for by in (1, 2, 3):
        copy2_x(by).start()

    wait_got(got1_y, 2)

    def sum1_y(i, carry):
        z_, xh_, xl_ = lax.div(i, 4), lax.rem(lax.div(i, 2), 2), lax.rem(i, 2)
        term_y[y, z_, xh_, xl_] = summed(
            term_y[y, z_, xh_, xl_], [got1_y[r, z_, xh_, xl_] for r in range(3)]
        ).astype(BF16)
        return carry

    lax.fori_loop(0, 16, sum1_y, 0)

    def copy2_y(by):
        return remote(
            term_y.at[y, flip(z, by)], got2_y.at[by - 1], rs_send.at[5, by - 1],
            rs_recv.at[5, by - 1], along_z(by),
        )

    for by in (1, 2, 3):
        copy2_y(by).start()

    for by in range(1, 8):
        slots(by, proj_slots, 1).wait_recv()
    pool[ROWS:, :] = proj_slots[...]
    og_copy.wait_send()
    pick(1, ROWS, ROWS + 8 * SLOT, og_pair, core)
    proj_copy = pltpu.make_async_copy(og_pair.at[core], proj_hbm, load_sem.at[0])
    proj_copy.start()

    wait_got(got2_x, 4)
    for z_ in range(4):
        term_x[xh, xl, y, z_] = summed(
            term_x[xh, xl, y, z_], [got2_x[r, z_] for r in range(3)]
        ).astype(BF16)

    def copy3_x(by):
        return remote(
            term_x.at[xh, xl, y, flip(z, by)], got3_x.at[by - 1], rs_send.at[6, by - 1],
            rs_recv.at[6, by - 1], along_z(by),
        )

    for by in (1, 2, 3):
        copy3_x(by).start()

    wait_got(got2_y, 5)
    for xh_ in range(2):
        for xl_ in range(2):
            term_y[y, z, xh_, xl_] = summed(
                term_y[y, z, xh_, xl_], [got2_y[r, xh_, xl_] for r in range(3)]
            ).astype(BF16)

    def copy3_y(by):
        return remote(
            term_y.at[y, z, lax.rem(xh + by // 2, 2), lax.rem(xl + by % 2, 2)], got3_y.at[by - 1],
            rs_send.at[7, by - 1], rs_recv.at[7, by - 1], along_x(by),
        )

    for by in (1, 2, 3):
        copy3_y(by).start()

    wait_got(got2_z, 3)
    for y_ in range(4):
        term_z[xh, z, xl, y_] = summed(
            term_z[xh, z, xl, y_], [got2_z[r, y_] for r in range(3)]
        ).astype(BF16)

    def copy3_z(by):
        return remote(
            term_z.at[xh, z, xl, flip(y, by)], got3_z.at[by - 1], rs_send.at[8, by - 1],
            rs_recv.at[8, by - 1], along_y(by),
        )

    for by in (1, 2, 3):
        copy3_z(by).start()

    wait_got(got3_x, 6)
    dw_rows[Z_ROWS : Z_ROWS + X_ROWS, :] = summed(
        term_x[xh, xl, y, z], [got3_x[r] for r in range(3)]
    ).astype(BF16)
    wait_got(got3_y, 7)
    dw_rows[Z_ROWS + X_ROWS :, :] = summed(
        term_y[y, z, xh, xl], [got3_y[r] for r in range(3)]
    ).astype(BF16)
    wait_got(got3_z, 8)
    dw_rows[:Z_ROWS, :] = summed(term_z[xh, z, xl, y], [got3_z[r] for r in range(3)]).astype(BF16)
    dw_copy = pltpu.make_async_copy(dw_rows, dw_hbm, load_sem.at[1])
    dw_copy.start()

    for by in range(4):
        for chunk in range(4):
            if by > 0:
                w_along_y(by, chunk).wait_send()
            w_along_x(by, chunk).wait_send()
        attn_copy(by).wait_send()
        grad_copy(by).wait_send()
    for by in range(1, 8):
        slots(by, proj_slots, 1).wait_send()
    for block in range(8):
        part_copy(block).wait_send()
    sent = (got1_z, got1_x, got1_y, got2_z, got2_x, got2_y, got3_x, got3_y, got3_z)
    for kind in range(9):
        for by in (1, 2, 3):
            all_of(sent[kind].at[by - 1], rs_send.at[kind, by - 1]).wait()
    for by in range(4):
        for which in range(3):
            store_copy(by, which).wait()
    proj_copy.wait()
    dw_copy.wait()


def row_tables(image_lengths, image_dest, image_offset):
    img_count = image_lengths.shape[1]
    dp_count = lax.axis_size("dp")
    fs_count = lax.axis_size("fsdp")
    dp_index = lax.axis_index("dp")
    fs_index = lax.axis_index("fsdp")
    starts = jnp.cumsum(image_lengths, axis=1) - image_lengths

    def group_view(table):
        return lax.dynamic_index_in_dim(
            table.reshape(dp_count, fs_count, img_count), fs_index, axis=1, keepdims=False
        )

    def own(table):
        return lax.dynamic_index_in_dim(table, dp_index, axis=0, keepdims=False)

    grp_len = group_view(image_lengths) // SLOT
    grp_start = group_view(starts) // SLOT
    grp_dest = group_view(image_dest)
    grp_off = group_view(image_offset) // SLOT
    own_len, own_start, own_dest, own_off = own(grp_len), own(grp_start), own(grp_dest), own(grp_off)
    peers = jnp.arange(dp_count, dtype=jnp.int32)
    unit_count = ROWS // SLOT
    units = jnp.arange(unit_count, dtype=jnp.int32)
    arriving = grp_dest == dp_index
    senders = peers[:, None]
    back = jnp.sum(jnp.where(arriving & (senders != dp_index), grp_off, 0), axis=1)
    home_base = jnp.where(own_dest == dp_index, own_off, unit_count + own_dest) - own_start
    inside = (units[None, :] >= own_start[:, None]) & (units[None, :] < (own_start + own_len)[:, None])
    home = jnp.sum(jnp.where(inside, home_base[:, None] + units[None, :], 0), axis=0)
    leaving = (own_dest[None, :] == peers[:, None]) & (own_dest[None, :] != dp_index)
    send = jnp.sum(jnp.where(leaving, own_start[None, :], 0), axis=1)
    source_base = jnp.where(senders == dp_index, grp_start, unit_count + senders) - grp_off
    covers = (
        arriving[:, :, None]
        & (units[None, None, :] >= grp_off[:, :, None])
        & (units[None, None, :] < (grp_off + grp_len)[:, :, None])
    )
    place = jnp.sum(
        jnp.where(covers, source_base[:, :, None] + units[None, None, :], 0), axis=(0, 1)
    )
    within = jnp.arange(SLOT, dtype=jnp.int32)

    def unit_rows(first):
        return (first[:, None] * SLOT + within[None, :]).reshape(-1)

    row_ids = jnp.arange(ROWS, dtype=jnp.int32)
    image = jnp.sum(jnp.where(row_ids[None, :] >= (own_start * SLOT)[:, None], 1, 0), axis=0)
    fill = (0, ROWS - dp_count * SLOT)
    columns = [
        unit_rows(home),
        unit_rows(place),
        image,
        jnp.pad(unit_rows(back), fill),
        jnp.pad(unit_rows(send), fill),
    ]
    return jnp.stack(columns, axis=1).astype(jnp.int32), image[None, :].astype(jnp.int32)


def shards(
    queries, key_vectors, value_vectors, image_lengths, image_dest, image_offset, out_weight, out_grad
):
    table, images = row_tables(image_lengths, image_dest, image_offset)
    any_space = pl.BlockSpec(memory_space=pl.ANY)
    rows = jax.ShapeDtypeStruct((ROWS, D), BF16)
    vmem = pltpu.VMEM
    dma = pltpu.SemaphoreType.DMA
    return pl.pallas_call(
        kernel,
        out_shape=(rows, rows, rows, rows, jax.ShapeDtypeStruct((SHARD, BLOCK), BF16)),
        in_specs=[pl.BlockSpec(memory_space=vmem)] * 2 + [any_space] * 5,
        out_specs=[any_space] * 5,
        scratch_shapes=[
            vmem((ROWS, D), BF16),
            vmem((ROWS, D), BF16),
            vmem((ROWS, D), BF16),
            vmem((8 * SHARD, D), BF16),
            vmem((ROWS + 8 * SLOT, D), BF16),
            vmem((8 * SLOT, D), BF16),
            vmem((8 * SLOT, D), BF16),
            vmem((2, ROWS, D), BF16),
            vmem((2, 4, ROWS, HALF), BF16),
            vmem((4, ROWS, HALF), BF16),
            vmem((4, HALF, 2 * ROWS), BF16),
            vmem((24, ROWS, ROWS), BF16),
            vmem((ROWS, ROWS), F32),
            vmem((ROWS, GROUP), BF16),
            vmem((4, ROWS, HALF), BF16),
            vmem((4, ROWS, HALF), BF16),
            vmem((4, ROWS, HALF), BF16),
            vmem((2, ROWS, BLOCK), F32),
            vmem((8, ROWS, BLOCK), BF16),
            vmem((8, ROWS, BLOCK), BF16),
            vmem((8 * SLOT, D), BF16),
            vmem((2, 4, 2, 4, Z_ROWS, BLOCK), BF16),
            vmem((2, 2, 4, 4, X_ROWS, BLOCK), BF16),
            vmem((4, 4, 2, 2, Y_ROWS, BLOCK), BF16),
            vmem((3, 2, 2, 4, Z_ROWS, BLOCK), BF16),
            vmem((3, 4, 4, X_ROWS, BLOCK), BF16),
            vmem((3, 4, 2, 2, Y_ROWS, BLOCK), BF16),
            vmem((3, 4, Z_ROWS, BLOCK), BF16),
            vmem((3, 4, X_ROWS, BLOCK), BF16),
            vmem((3, 2, 2, Y_ROWS, BLOCK), BF16),
            vmem((3, Z_ROWS, BLOCK), BF16),
            vmem((3, X_ROWS, BLOCK), BF16),
            vmem((3, Y_ROWS, BLOCK), BF16),
            vmem((SHARD, BLOCK), BF16),
            dma((5,)),
            dma((3, 4)),
            dma((3, 4)),
            dma((3, 4)),
            dma((4, 4)),
            dma((4, 4)),
            dma((2, 7)),
            dma((2, 7)),
            dma((4, 8)),
            dma((4, 8)),
            dma((9, 3)),
            dma((9, 3)),
        ],
        compiler_params=pltpu.CompilerParams(
            collective_id=0, has_side_effects=True, vmem_limit_bytes=63 * 2**20
        ),
        name="attention_step",
    )(table, images, queries, key_vectors, value_vectors, out_weight, out_grad)


def solution(mesh):
    rows = P(("dp", "fsdp"), None)
    return jax.shard_map(
        shards,
        mesh=mesh,
        in_specs=(rows, rows, rows, P(), P(), P(), P("fsdp", None), rows),
        out_specs=(rows, rows, rows, rows, P("fsdp", "dp")),
        check_vma=False,
    )
```

time: 464 us -> 167 us (0.36); the launches traced: 456 us -> 167 us
  waiting for transfers between devices: 280 us -> 0 us
  Pallas kernels: 0 us -> 149 us
  matrix products: 75.7 us -> 0 us
  local copies, waits for them, and re-layouts: 42.1 us -> 14.5 us
  other arithmetic: 29.1 us -> 2.48 us
  starting transfers between devices: 14.7 us -> 0 us
  between operations: 14.5 us -> 0.74 us
    reduce_scatter x1 -> x0, waiting for transfers between devices: 179 us -> none  [shards(): lax.psum_scatter((lax.dot_general(attn, grad_rows, (((0,), (0,)), ((), ()...]
    pallas_call x0 -> x1, Pallas kernels: none -> 149 us  [shards(): pl.pallas_call(kernel, out_shape=(rows, rows, rows, rows, jax.ShapeDtypeS...]
    dot_general x9 -> x0, matrix products: 75.7 us -> none  [the longest x3 28.1 us: attention(): scores = jnp.einsum('ahd,bhd->hab', query_heads, key_heads) * HD ** (-0.5)]
    all_gather x1 -> x0, waiting for transfers between devices: 57.8 us -> none  [shards(): full_weight = lax.all_gather(out_weight, 'fsdp', axis=0, tiled=True)]
    unnamed x4 -> x0, waiting for transfers between devices: 42.8 us -> none
    gather x4 -> x0, local copies, waits for them, and re-layouts: 21.6 us -> none  [the longest x2 17 us: from_pool(): return jnp.take(pooled, row_source, axis=0)]
    sub x2 -> x1, other arithmetic: 16.1 us -> 0.69 us  [row_tables(): starts = jnp.cumsum(image_lengths, axis=1) - image_lengths]
    all_to_all x2 -> x0, starting transfers between devices: 14.6 us -> none  [the longest x1 8.32 us: shards(): lax.all_to_all(take_slots(out_grad, back_source, back_valid), 'dp', split...]
  transfers between devices with their start and end apart: 5 -> 0, of which waited for: 3 -> 0; matrix products, arithmetic and copies ran while one was open for 23% -> 0% of each run, Pallas kernels for 0% -> 0%
where the time goes in v2:
time: 167 us
  Pallas kernels  149 us (89%)
  local copies, waits for them, and re-layouts  14.5 us (9%)
  other arithmetic  2.48 us (1%)
    pallas_call x1, Pallas kernels, shards(): pl.pallas_call(kernel, out_shape=(rows, rows, rows, rows, jax.ShapeDtypeS...  149 us
    unnamed x13, local copies, waits for them, and re-layouts  9.03 us

profile of v2, /device:TPU:1, one launch (start us, length us, event | category | flops | bytes accessed | tf_op | source)
XLA Modules:
  0.0 167.0 jit_solution(11416829103771285084)
XLA Ops:
  0.7 0.7 reduce_window_sum.11
  1.4 0.7 sub.31
  2.2 0.1 copy.36
  2.4 0.8 reshape.292
  3.1 0.3 dynamic-slice_reduce_fusion
  3.5 0.1 copy.45
  3.6 0.1 copy.39
  3.8 0.8 reshape.293
  4.5 0.8 reshape.291
  5.4 0.1 copy.38
  5.5 0.2 select_reduce_fusion.3
  6.0 0.1 copy.37
  6.3 0.1 select_reduce_fusion.2
  6.6 0.6 broadcast_in_dim.53.images
  7.4 0.1 select_reduce_fusion
  7.9 0.8 copy.44.table
  8.7 149.2 %attention_step.1 = (bf16[288,3072]{1,0:T(8,128)(2,1)}, bf16[288,3072]{1,0:T(8,128)(2,1)}, bf16[288,3072]{1,0:T(8,128)(2,1)}, bf16[288,3072]{1,0:T(8,128)(2,1)}, bf16[192,384]{1,0:T(8,128)(2,1)}) custom-call(s32[288,5]{1,0:T(8,128)} %copy.44.table, s32[1,288]{1,0:T(1,128)} %broadcast_in_dim.53.images, bf16[288,3072]{1,0:T(8,128)(2,1)} %q_hbm.1, ...), custom_call_target="tpu_custom_call" | custom-call | tf_op jit(solution)/shard_map/attention_step/pallas_call | solution.py:680
  157.9 2.9 %copy.51 = bf16[288,3072]{1,0:T(8,128)(2,1)} copy(bf16[288,3072]{1,0:T(8,128)(2,1)} %get-tuple-element.24) | data formatting | bytes 3538944
  160.9 1.2 copy.52
  162.1 0.9 copy-done.1
  163.0 1.2 copy.53
  164.2 0.9 copy-done
  165.1 1.2 copy.54
  166.3 0.7 copy.55
  (39 shorter events, 1.5 us)
Async XLA Ops:
  157.9 2.9 %copy-start.2 = (bf16[288,3072]{1,0:T(8,128)(2,1)S(1)}, bf16[288,3072]{1,0:T(8,128)(2,1)}, u32[]{:S(2)}) copy-start(bf16[288,3072]{1,0:T(8,128)(2,1)} %get-tuple-element.25) | copy-start | bytes 5308420
  160.9 2.1 %copy-start.1 = (bf16[288,3072]{1,0:T(8,128)(2,1)S(1)}, bf16[288,3072]{1,0:T(8,128)(2,1)}, u32[]{:S(2)}) copy-start(bf16[288,3072]{1,0:T(8,128)(2,1)} %get-tuple-element.26) | copy-start | bytes 5308420
  163.0 2.1 %copy-start = (bf16[288,3072]{1,0:T(8,128)(2,1)S(1)}, bf16[288,3072]{1,0:T(8,128)(2,1)}, u32[]{:S(2)}) copy-start(bf16[288,3072]{1,0:T(8,128)(2,1)} %get-tuple-element.27) | copy-start | bytes 5308420
  165.1 1.2 copy-start.3

commit v3 on v2

--- a/solution.py
+++ b/solution.py
@@ -17,7 +17,7 @@
 SHARD = 192
 CHUNK = 48
 BLOCK = 384
-Z_ROWS, X_ROWS, Y_ROWS = 96, 48, 48
+PIPES = ((0, 64, "zyx", 1), (64, 64, "zxy", 3), (128, 32, "yzx", 1), (160, 32, "yxz", 3))
 SCALE = HD ** (-0.5)
 
 
@@ -66,18 +66,26 @@
     part_out,
     part_in,
     proj_slots,
-    term_z,
-    term_x,
-    term_y,
-    got1_z,
-    got1_x,
-    got1_y,
-    got2_z,
-    got2_x,
-    got2_y,
-    got3_z,
-    got3_x,
-    got3_y,
+    term_0,
+    term_1,
+    term_2,
+    term_3,
+    pair_0,
+    pair_1,
+    pair_2,
+    pair_3,
+    quad_0,
+    quad_1,
+    quad_2,
+    quad_3,
+    next_0,
+    next_1,
+    next_2,
+    next_3,
+    last_0,
+    last_1,
+    last_2,
+    last_3,
     dw_rows,
     load_sem,
     store_sem,
@@ -167,26 +175,37 @@
         return pl.ds(pl.multiple_of((y_ * 2 + xl_) * SHARD + chunk * CHUNK, CHUNK), CHUNK)
 
     def w_along_y(by, chunk):
-        rows = weight.at[shard_rows(y, xl, chunk)]
-        return remote(
-            rows, rows, wy_send.at[by - 1, chunk], wy_recv.at[by - 1, chunk], along_y(by)
+        via = (1 if chunk < 2 else 3) if by == 2 else 0
+        rows = weight.at[shard_rows(flip(y, via), xl, chunk)]
+        return remote(
+            rows,
+            rows,
+            wy_send.at[by - 1, chunk],
+            wy_recv.at[by - 1, chunk],
+            along_y(4 - via if by == 2 else by),
         )
 
     def w_along_x(by, chunk):
         rows = weight.at[shard_rows(flip(y, by), xl, chunk)]
         return remote(
-            rows, rows, wx_send.at[by, chunk], wx_recv.at[by, chunk], along_x(1 if chunk < 2 else 3)
+            rows,
+            rows,
+            wx_send.at[by, chunk],
+            wx_recv.at[by, chunk],
+            along_x(1 if chunk % 2 == 0 else 3),
         )
 
     def forward(by, chunk):
         w_along_y(by, chunk).wait_recv()
+        if by == (1 if chunk < 2 else 3):
+            w_along_y(2, chunk).start()
         w_along_x(by, chunk).start()
 
     loads[0].wait()
     for step in range(4):
-        w_along_y(1, (0, 2, 1, 3)[step]).start()
-        w_along_y(3, (2, 0, 3, 1)[step]).start()
-        w_along_x(0, (0, 2, 1, 3)[step]).start()
+        w_along_y(1, step).start()
+        w_along_y(3, 3 - step).start()
+        w_along_x(0, step).start()
 
     def unit(index):
         return pl.ds(pl.multiple_of(index * SLOT, SLOT), SLOT)
@@ -252,7 +271,7 @@
     attend(0)
     attend(1)
     forward(1, 0)
-    forward(3, 2)
+    forward(3, 3)
     attend(2)
 
     for by in range(1, 8):
@@ -264,10 +283,8 @@
     )
     og_copy.start()
     attend(3)
-    forward(1, 2)
-    forward(3, 0)
-    w_along_y(2, 0).start()
-    w_along_y(2, 2).start()
+    forward(1, 1)
+    forward(3, 2)
 
     for group in range(4):
         attn_copy(group).wait_recv()
@@ -276,60 +293,64 @@
 
     grad_scale = (ROWS * 128) ** (-0.5)
 
-    def copy1_z(xh_, z_, by):
-        return remote(
-            term_z.at[xh_, z_], got1_z.at[by - 1, xh_], rs_send.at[0, by - 1], rs_recv.at[0, by - 1],
-            device(xh, xl, y, z_, core),
-        )
-
-    def copy1_x(xh_, xl_, z_, by):
-        return remote(
-            term_x.at[xh_, xl_, :, z_], got1_x.at[by - 1, :, z_], rs_send.at[1, by - 1],
-            rs_recv.at[1, by - 1], device(xh_, xl_, y, z, core),
-        )
-
-    def copy1_y(xh_, y_, z_, by):
-        return remote(
-            term_y.at[y_, z_, xh_], got1_y.at[by - 1, z_, xh_], rs_send.at[2, by - 1],
-            rs_recv.at[2, by - 1], device(xh, xl, y_, z, core),
-        )
-
-    def one_term(i, carry):
-        by_z, by_xh = 3 - lax.div(i, 2), 1 - lax.rem(i, 2)
-        z_ = lax.rem(lax.div(z, 2) + lax.div(by_z, 2), 2) * 2 + lax.rem(z + by_z, 2)
-        xh_ = lax.rem(xh + by_xh, 2)
-        cols = pl.ds(pl.multiple_of((xh_ * 4 + z_) * BLOCK, BLOCK), BLOCK)
-        grads = og_pair[:, :, cols].reshape(2 * ROWS, BLOCK)
-        for group in range(4):
-            term = (contract(attn_t[group], grads, 1, 0) * grad_scale).astype(BF16)
-            for xl_ in range(2):
-                at = xl_ * SHARD
-                term_z[xh_, z_, xl_, group] = term[at : at + Z_ROWS]
-                term_x[xh_, xl_, group, z_] = term[at + Z_ROWS : at + Z_ROWS + X_ROWS]
-                term_y[group, z_, xh_, xl_] = term[at + Z_ROWS + X_ROWS : at + SHARD]
-
-        @pl.when(by_z > 0)
-        def _():
-            copy1_z(xh_, z_, by_z).start()
-
-        for by_xl in range(2):
-
-            @pl.when(by_xh * 2 + by_xl > 0)
-            def _():
-                copy1_x(xh_, lax.rem(xl + by_xl, 2), z_, by_xh * 2 + by_xl).start()
-
-        for by_y in (1, 2, 3):
-            copy1_y(xh_, flip(y, by_y), z_, by_y).start()
-        return carry
-
-    lax.fori_loop(0, 4, one_term, 0)
-    forward(1, 1)
-    forward(3, 3)
-    w_along_y(2, 1).start()
-    w_along_y(2, 3).start()
-    lax.fori_loop(4, 8, one_term, 0)
+    x = xh * 2 + xl
+    here_on = {"x": x, "y": y, "z": z}
+    along = {"x": along_x, "y": along_y, "z": along_z}
+    terms = (term_0, term_1, term_2, term_3)
+    pairs = (pair_0, pair_1, pair_2, pair_3)
+    quads = (quad_0, quad_1, quad_2, quad_3)
+    nexts = (next_0, next_1, next_2, next_3)
+    lasts = (last_0, last_1, last_2, last_3)
+
+    def first_copy(pipe, by, z_):
+        near = PIPES[pipe][3]
+        slot = 0 if by == 2 else 1
+        term, pair = terms[pipe], pairs[pipe].at[slot]
+        if pipe < 2:
+            src, dst = term.at[z_], pair
+        elif pipe == 2:
+            src, dst = term.at[flip(y, by), z_], pair.at[z_]
+        else:
+            src, dst = term.at[flip(y, by), :, z_], pair.at[:, z_]
+        return remote(
+            src, dst, rs_send.at[pipe, slot], rs_recv.at[pipe, slot], along[PIPES[pipe][2][0]](near)
+        )
+
+    def compute_terms(by_z):
+        z_ = flip(z, by_z)
+
+        def one_term(by_xh, carry):
+            xh_ = lax.rem(xh + 1 + by_xh, 2)
+            cols = pl.ds(pl.multiple_of((xh_ * 4 + z_) * BLOCK, BLOCK), BLOCK)
+            grads = og_pair[:, :, cols].reshape(2 * ROWS, BLOCK)
+            for y_ in range(4):
+                term = (contract(attn_t[y_], grads, 1, 0) * grad_scale).astype(BF16)
+                for xl_ in range(2):
+                    x_ = xh_ * 2 + xl_
+                    places = ((z_, y_, x_), (z_, x_, y_), (y_, z_, x_), (y_, x_, z_))
+                    for (first_row, count, _, _), buffer, place in zip(PIPES, terms, places):
+                        at = xl_ * SHARD + first_row
+                        buffer[place] = term[at : at + count]
+            return carry
+
+        lax.fori_loop(0, 2, one_term, 0)
+        for pipe in range(4):
+            near = PIPES[pipe][3]
+            if pipe < 2:
+                if by_z in (2, near):
+                    first_copy(pipe, by_z, z_).start()
+            else:
+                first_copy(pipe, 2, z_).start()
+                first_copy(pipe, near, z_).start()
+
+    compute_terms(2)
+    forward(1, 2)
+    forward(3, 1)
+    compute_terms(1)
+    compute_terms(3)
     forward(1, 3)
-    forward(3, 1)
+    forward(3, 0)
+    compute_terms(0)
 
     def grad_copy(by):
         return remote(
@@ -393,16 +414,117 @@
         for which in range(3):
             store_copy(by, which).start()
 
+    def all_of(buffer, sem):
+        return pltpu.make_async_copy(buffer, buffer, sem)
+
+    def summed(own, others):
+        total = own.astype(F32)
+        for other in others:
+            total += other.astype(F32)
+        return total.astype(BF16)
+
+    def second_copy(pipe, half):
+        _, _, axes, near = PIPES[pipe]
+        rows = pl.ds(half * 2, 2)
+        return remote(
+            terms[pipe].at[flip(here_on[axes[0]], 4 - near), rows],
+            quads[pipe].at[rows],
+            rs_send.at[pipe, 2],
+            rs_recv.at[pipe, 2],
+            along[axes[0]](4 - near),
+        )
+
+    def pipe_second(pipe):
+        term, pair = terms[pipe], pairs[pipe]
+        far = flip(here_on[PIPES[pipe][2][0]], 4 - PIPES[pipe][3])
+        all_of(pair.at[0], rs_recv.at[pipe, 0]).wait()
+        for half in range(2):
+
+            def one_block(i, carry):
+                second, third = half * 2 + lax.div(i, 4), lax.rem(i, 4)
+                term[far, second, third] = summed(
+                    term[far, second, third], [pair[0, second, third]]
+                )
+                return carry
+
+            lax.fori_loop(0, 8, one_block, 0)
+            second_copy(pipe, half).start()
+
+    def third_copy(pipe, by):
+        axes = PIPES[pipe][2]
+        return remote(
+            terms[pipe].at[here_on[axes[0]], flip(here_on[axes[1]], by)],
+            nexts[pipe].at[by - 1],
+            rs_send.at[pipe, 2 + by],
+            rs_recv.at[pipe, 2 + by],
+            along[axes[1]](by),
+        )
+
+    def pipe_third(pipe):
+        term, pair, quad = terms[pipe], pairs[pipe], quads[pipe]
+        own = here_on[PIPES[pipe][2][0]]
+        all_of(pair.at[1], rs_recv.at[pipe, 1]).wait()
+        all_of(quad, rs_recv.at[pipe, 2]).wait()
+
+        def one_block(i, carry):
+            second, third = lax.div(i, 4), lax.rem(i, 4)
+            term[own, second, third] = summed(
+                term[own, second, third], [pair[1, second, third], quad[second, third]]
+            )
+            return carry
+
+        lax.fori_loop(0, 16, one_block, 0)
+        for by in (2, 1, 3):
+            third_copy(pipe, by).start()
+
+    def fourth_copy(pipe, by):
+        axes = PIPES[pipe][2]
+        return remote(
+            terms[pipe].at[here_on[axes[0]], here_on[axes[1]], flip(here_on[axes[2]], by)],
+            lasts[pipe].at[by - 1],
+            rs_send.at[pipe, 5 + by],
+            rs_recv.at[pipe, 5 + by],
+            along[axes[2]](by),
+        )
+
+    def pipe_fourth(pipe):
+        term, arrived = terms[pipe], nexts[pipe]
+        axes = PIPES[pipe][2]
+        own = here_on[axes[0]], here_on[axes[1]]
+        for by in (1, 2, 3):
+            third_copy(pipe, by).wait_recv()
+
+        def one_block(third, carry):
+            place = own + (third,)
+            term[place] = summed(term[place], [arrived[r, third] for r in range(3)])
+            return carry
+
+        lax.fori_loop(0, 4, one_block, 0)
+        for by in (2, 1, 3):
+            fourth_copy(pipe, by).start()
+
+    def pipe_last(pipe):
+        first_row, count, axes, _ = PIPES[pipe]
+        for by in (1, 2, 3):
+            fourth_copy(pipe, by).wait_recv()
+        dw_rows[first_row : first_row + count, :] = summed(
+            terms[pipe][tuple(here_on[axis] for axis in axes)], [lasts[pipe][r] for r in range(3)]
+        )
+
     attn_grad(0)
     attend_back(0)
     forward(2, 0)
-    forward(2, 2)
+    forward(2, 3)
     attn_grad(1)
     attend_back(1)
     forward(2, 1)
+    forward(2, 2)
+    pipe_second(0)
+    pipe_second(1)
     attn_grad(3)
-    forward(2, 3)
     attend_back(3)
+    pipe_second(2)
+    pipe_second(3)
     attn_grad(2)
 
     def part_copy(block):
@@ -447,79 +569,8 @@
 
     attend_back(2)
 
-    def all_of(buffer, sem):
-        return pltpu.make_async_copy(buffer, buffer, sem)
-
-    def summed(own, others):
-        total = own.astype(F32)
-        for other in others:
-            total += other.astype(F32)
-        return total
-
-    def wait_got(buffer, kind):
-        for by in (1, 2, 3):
-            all_of(buffer.at[by - 1], rs_recv.at[kind, by - 1]).wait()
-
-    wait_got(got1_z, 0)
-
-    def sum1_z(i, carry):
-        xh_, xl_, y_ = lax.div(i, 8), lax.rem(lax.div(i, 4), 2), lax.rem(i, 4)
-        term_z[xh_, z, xl_, y_] = summed(
-            term_z[xh_, z, xl_, y_], [got1_z[r, xh_, xl_, y_] for r in range(3)]
-        ).astype(BF16)
-        return carry
-
-    lax.fori_loop(0, 16, sum1_z, 0)
-
-    def copy2_z(by):
-        xh_, xl_ = lax.rem(xh + by // 2, 2), lax.rem(xl + by % 2, 2)
-        return remote(
-            term_z.at[xh_, z, xl_], got2_z.at[by - 1], rs_send.at[3, by - 1], rs_recv.at[3, by - 1],
-            along_x(by),
-        )
-
-    for by in (1, 2, 3):
-        copy2_z(by).start()
-
-    wait_got(got1_x, 1)
-
-    def sum1_x(i, carry):
-        y_, z_ = lax.div(i, 4), lax.rem(i, 4)
-        term_x[xh, xl, y_, z_] = summed(
-            term_x[xh, xl, y_, z_], [got1_x[r, y_, z_] for r in range(3)]
-        ).astype(BF16)
-        return carry
-
-    lax.fori_loop(0, 16, sum1_x, 0)
-
-    def copy2_x(by):
-        return remote(
-            term_x.at[xh, xl, flip(y, by)], got2_x.at[by - 1], rs_send.at[4, by - 1],
-            rs_recv.at[4, by - 1], along_y(by),
-        )
-
-    for by in (1, 2, 3):
-        copy2_x(by).start()
-
-    wait_got(got1_y, 2)
-
-    def sum1_y(i, carry):
-        z_, xh_, xl_ = lax.div(i, 4), lax.rem(lax.div(i, 2), 2), lax.rem(i, 2)
-        term_y[y, z_, xh_, xl_] = summed(
-            term_y[y, z_, xh_, xl_], [got1_y[r, z_, xh_, xl_] for r in range(3)]
-        ).astype(BF16)
-        return carry
-
-    lax.fori_loop(0, 16, sum1_y, 0)
-
-    def copy2_y(by):
-        return remote(
-            term_y.at[y, flip(z, by)], got2_y.at[by - 1], rs_send.at[5, by - 1],
-            rs_recv.at[5, by - 1], along_z(by),
-        )
-
-    for by in (1, 2, 3):
-        copy2_y(by).start()
+    for pipe in (2, 3, 0, 1):
+        pipe_third(pipe)
 
     for by in range(1, 8):
         slots(by, proj_slots, 1).wait_recv()
@@ -529,62 +580,10 @@
     proj_copy = pltpu.make_async_copy(og_pair.at[core], proj_hbm, load_sem.at[0])
     proj_copy.start()
 
-    wait_got(got2_x, 4)
-    for z_ in range(4):
-        term_x[xh, xl, y, z_] = summed(
-            term_x[xh, xl, y, z_], [got2_x[r, z_] for r in range(3)]
-        ).astype(BF16)
-
-    def copy3_x(by):
-        return remote(
-            term_x.at[xh, xl, y, flip(z, by)], got3_x.at[by - 1], rs_send.at[6, by - 1],
-            rs_recv.at[6, by - 1], along_z(by),
-        )
-
-    for by in (1, 2, 3):
-        copy3_x(by).start()
-
-    wait_got(got2_y, 5)
-    for xh_ in range(2):
-        for xl_ in range(2):
-            term_y[y, z, xh_, xl_] = summed(
-                term_y[y, z, xh_, xl_], [got2_y[r, xh_, xl_] for r in range(3)]
-            ).astype(BF16)
-
-    def copy3_y(by):
-        return remote(
-            term_y.at[y, z, lax.rem(xh + by // 2, 2), lax.rem(xl + by % 2, 2)], got3_y.at[by - 1],
-            rs_send.at[7, by - 1], rs_recv.at[7, by - 1], along_x(by),
-        )
-
-    for by in (1, 2, 3):
-        copy3_y(by).start()
-
-    wait_got(got2_z, 3)
-    for y_ in range(4):
-        term_z[xh, z, xl, y_] = summed(
-            term_z[xh, z, xl, y_], [got2_z[r, y_] for r in range(3)]
-        ).astype(BF16)
-
-    def copy3_z(by):
-        return remote(
-            term_z.at[xh, z, xl, flip(y, by)], got3_z.at[by - 1], rs_send.at[8, by - 1],
-            rs_recv.at[8, by - 1], along_y(by),
-        )
-
-    for by in (1, 2, 3):
-        copy3_z(by).start()
-
-    wait_got(got3_x, 6)
-    dw_rows[Z_ROWS : Z_ROWS + X_ROWS, :] = summed(
-        term_x[xh, xl, y, z], [got3_x[r] for r in range(3)]
-    ).astype(BF16)
-    wait_got(got3_y, 7)
-    dw_rows[Z_ROWS + X_ROWS :, :] = summed(
-        term_y[y, z, xh, xl], [got3_y[r] for r in range(3)]
-    ).astype(BF16)
-    wait_got(got3_z, 8)
-    dw_rows[:Z_ROWS, :] = summed(term_z[xh, z, xl, y], [got3_z[r] for r in range(3)]).astype(BF16)
+    for pipe in (2, 3, 0, 1):
+        pipe_fourth(pipe)
+    for pipe in (2, 3, 0, 1):
+        pipe_last(pipe)
     dw_copy = pltpu.make_async_copy(dw_rows, dw_hbm, load_sem.at[1])
     dw_copy.start()
 
@@ -599,10 +598,13 @@
         slots(by, proj_slots, 1).wait_send()
     for block in range(8):
         part_copy(block).wait_send()
-    sent = (got1_z, got1_x, got1_y, got2_z, got2_x, got2_y, got3_x, got3_y, got3_z)
-    for kind in range(9):
+    for pipe in range(4):
+        for slot in range(2):
+            all_of(pairs[pipe].at[slot], rs_send.at[pipe, slot]).wait()
+        all_of(quads[pipe], rs_send.at[pipe, 2]).wait()
         for by in (1, 2, 3):
-            all_of(sent[kind].at[by - 1], rs_send.at[kind, by - 1]).wait()
+            third_copy(pipe, by).wait_send()
+            fourth_copy(pipe, by).wait_send()
     for by in range(4):
         for which in range(3):
             store_copy(by, which).wait()
@@ -704,18 +706,11 @@
             vmem((8, ROWS, BLOCK), BF16),
             vmem((8, ROWS, BLOCK), BF16),
             vmem((8 * SLOT, D), BF16),
-            vmem((2, 4, 2, 4, Z_ROWS, BLOCK), BF16),
-            vmem((2, 2, 4, 4, X_ROWS, BLOCK), BF16),
-            vmem((4, 4, 2, 2, Y_ROWS, BLOCK), BF16),
-            vmem((3, 2, 2, 4, Z_ROWS, BLOCK), BF16),
-            vmem((3, 4, 4, X_ROWS, BLOCK), BF16),
-            vmem((3, 4, 2, 2, Y_ROWS, BLOCK), BF16),
-            vmem((3, 4, Z_ROWS, BLOCK), BF16),
-            vmem((3, 4, X_ROWS, BLOCK), BF16),
-            vmem((3, 2, 2, Y_ROWS, BLOCK), BF16),
-            vmem((3, Z_ROWS, BLOCK), BF16),
-            vmem((3, X_ROWS, BLOCK), BF16),
-            vmem((3, Y_ROWS, BLOCK), BF16),
+            *[vmem((4, 4, 4, count, BLOCK), BF16) for _, count, _, _ in PIPES],
+            *[vmem((2, 4, 4, count, BLOCK), BF16) for _, count, _, _ in PIPES],
+            *[vmem((4, 4, count, BLOCK), BF16) for _, count, _, _ in PIPES],
+            *[vmem((3, 4, count, BLOCK), BF16) for _, count, _, _ in PIPES],
+            *[vmem((3, count, BLOCK), BF16) for _, count, _, _ in PIPES],
             vmem((SHARD, BLOCK), BF16),
             dma((5,)),
             dma((3, 4)),
@@ -727,8 +722,8 @@
             dma((2, 7)),
             dma((4, 8)),
             dma((4, 8)),
-            dma((9, 3)),
-            dma((9, 3)),
+            dma((4, 9)),
+            dma((4, 9)),
         ],
         compiler_params=pltpu.CompilerParams(
             collective_id=0, has_side_effects=True, vmem_limit_bytes=63 * 2**20

time: 167 us -> 139 us (0.83)
  Pallas kernels: 149 us -> 121 us
    pallas_call x1, Pallas kernels: 149 us -> 121 us  [shards(): pl.pallas_call(kernel, out_shape=(rows, rows, rows, rows, jax.ShapeDtypeS...]
where the time goes in v3:
time: 139 us; the launch traced here: 138 us
  Pallas kernels  121 us (87%)
  local copies, waits for them, and re-layouts  14.5 us (10%)
  other arithmetic  2.48 us (2%)
    pallas_call x1, Pallas kernels, shards(): pl.pallas_call(kernel, out_shape=(rows, rows, rows, rows, jax.ShapeDtypeS...  121 us
    unnamed x13, local copies, waits for them, and re-layouts  9.03 us

profile of v3, /device:TPU:1, one launch (start us, length us, event | category | flops | bytes accessed | tf_op | source)
XLA Modules:
  0.0 138.5 jit_solution(12402646428622642144)
XLA Ops:
  0.7 0.7 reduce_window_sum.11
  1.4 0.7 sub.31
  2.2 0.1 copy.36
  2.4 0.8 reshape.292
  3.1 0.3 dynamic-slice_reduce_fusion
  3.5 0.1 copy.45
  3.6 0.1 copy.39
  3.8 0.8 reshape.293
  4.5 0.8 reshape.291
  5.4 0.1 copy.38
  5.5 0.2 select_reduce_fusion.3
  6.0 0.1 copy.37
  6.3 0.1 select_reduce_fusion.2
  6.6 0.6 broadcast_in_dim.53.images
  7.4 0.1 select_reduce_fusion
  7.9 0.8 copy.44.table
  8.7 120.7 %attention_step.1 = (bf16[288,3072]{1,0:T(8,128)(2,1)}, bf16[288,3072]{1,0:T(8,128)(2,1)}, bf16[288,3072]{1,0:T(8,128)(2,1)}, bf16[288,3072]{1,0:T(8,128)(2,1)}, bf16[192,384]{1,0:T(8,128)(2,1)}) custom-call(s32[288,5]{1,0:T(8,128)} %copy.44.table, s32[1,288]{1,0:T(1,128)} %broadcast_in_dim.53.images, bf16[288,3072]{1,0:T(8,128)(2,1)} %q_hbm.1, ...), custom_call_target="tpu_custom_call" | custom-call | tf_op jit(solution)/shard_map/attention_step/pallas_call | solution.py:682
  129.5 2.9 %copy.51 = bf16[288,3072]{1,0:T(8,128)(2,1)} copy(bf16[288,3072]{1,0:T(8,128)(2,1)} %get-tuple-element.24) | data formatting | bytes 3538944
  132.4 1.2 copy.52
  133.6 0.9 copy-done.1
  134.5 1.2 copy.53
  135.7 0.9 copy-done
  136.6 1.2 copy.54
  137.8 0.7 copy.55
  (39 shorter events, 1.5 us)
Async XLA Ops:
  129.4 2.9 %copy-start.2 = (bf16[288,3072]{1,0:T(8,128)(2,1)S(1)}, bf16[288,3072]{1,0:T(8,128)(2,1)}, u32[]{:S(2)}) copy-start(bf16[288,3072]{1,0:T(8,128)(2,1)} %get-tuple-element.25) | copy-start | bytes 5308420
  132.4 2.1 %copy-start.1 = (bf16[288,3072]{1,0:T(8,128)(2,1)S(1)}, bf16[288,3072]{1,0:T(8,128)(2,1)}, u32[]{:S(2)}) copy-start(bf16[288,3072]{1,0:T(8,128)(2,1)} %get-tuple-element.26) | copy-start | bytes 5308420
  134.5 2.1 %copy-start = (bf16[288,3072]{1,0:T(8,128)(2,1)S(1)}, bf16[288,3072]{1,0:T(8,128)(2,1)}, u32[]{:S(2)}) copy-start(bf16[288,3072]{1,0:T(8,128)(2,1)} %get-tuple-element.27) | copy-start | bytes 5308420
  136.6 1.2 copy-start.3

commit v4 on v3

--- a/solution.py
+++ b/solution.py
@@ -33,7 +33,6 @@
 
 
 def kernel(
-    table,
     images,
     q_hbm,
     k_hbm,
@@ -87,6 +86,7 @@
     last_2,
     last_3,
     dw_rows,
+    table,
     load_sem,
     store_sem,
     wy_send,
@@ -150,7 +150,50 @@
     for peer in peers:
         pl.semaphore_signal(barrier, inc=1, device_id=peer, device_id_type=MESH)
 
-    bias[...] = jnp.where(table[:, 2:3] == images[...], 0.0, -1e30).astype(F32)
+    width = images.shape[1] // 3
+
+    def images_of(dp_):
+        rows = pl.ds(dp_ * 16 + fs, 1)
+        length, dest, offset = (images[rows, i * width : (i + 1) * width] for i in range(3))
+        lane = lax.broadcasted_iota(jnp.int32, length.shape, 1)
+        start = jnp.zeros_like(length)
+        for image in range(length.shape[1] - 1):
+            start += jnp.where(lane > image, length[:, image : image + 1], 0)
+        return length, dest, offset, start
+
+    def sum_lanes(hit, value):
+        return jnp.sum(jnp.where(hit, value, 0), axis=1, keepdims=True)
+
+    length, dest, offset, start = images_of(dp)
+    row = lax.broadcasted_iota(jnp.int32, (ROWS, 1), 0)
+    inside = (row >= start) & (row < start + length)
+    table[:, 0:1] = sum_lanes(
+        inside, jnp.where(dest == dp, offset, ROWS + SLOT * dest) - start + row
+    )
+    slot_row = lax.broadcasted_iota(jnp.int32, (8 * SLOT, 1), 0)
+    slot, in_slot = lax.div(slot_row, SLOT), lax.rem(slot_row, SLOT)
+    table[: 8 * SLOT, 3:4] = (
+        sum_lanes((dest == slot) & (dest != dp), start + in_slot + 1) - 1
+    )
+    columns = lax.broadcasted_iota(jnp.int32, (1, ROWS), 1)
+    row_image = jnp.zeros((ROWS, 1), jnp.int32)
+    column_image = jnp.zeros((1, ROWS), jnp.int32)
+    for image in range(1, length.shape[1]):
+        first = start[:, image : image + 1]
+        row_image += jnp.where(row >= first, 1, 0)
+        column_image += jnp.where(columns >= first, 1, 0)
+    bias[...] = jnp.where(row_image == column_image, 0.0, -1e30).astype(F32)
+
+    senders = [images_of(sender) for sender in range(8)]
+    length, dest, offset, start = [jnp.concatenate(list(part), axis=1) for part in zip(*senders)]
+    sender = lax.div(lax.broadcasted_iota(jnp.int32, length.shape, 1), width)
+    covers = (dest == dp) & (row >= offset) & (row < offset + length)
+    table[:, 1:2] = sum_lanes(
+        covers, jnp.where(sender == dp, start, ROWS + SLOT * sender) - offset + row
+    )
+    table[: 8 * SLOT, 2:3] = (
+        sum_lanes((sender == slot) & (dest == dp) & (sender != dp), offset + in_slot + 1) - 1
+    )
 
     def pick(column, out_rows, in_rows, dst, dst_core=None):
         chosen = lax.broadcasted_iota(jnp.int32, (out_rows, in_rows), 1) == (
@@ -221,7 +264,7 @@
         )
 
     loads[1].wait()
-    pick(3, 8 * SLOT, ROWS, slot_out)
+    pick(2, 8 * SLOT, ROWS, slot_out)
     own_slot = jnp.zeros((SLOT, D), BF16)
     og_slots[unit(dp), :] = own_slot
     proj_slots[unit(dp), :] = own_slot
@@ -563,7 +606,7 @@
 
     for by in range(1, 8):
         slots(by, og_slots, 0).wait_send()
-    pick(4, 8 * SLOT, ROWS, slot_out)
+    pick(3, 8 * SLOT, ROWS, slot_out)
     for by in range(1, 8):
         slots(by, proj_slots, 1).start()
 
@@ -612,77 +655,51 @@
     dw_copy.wait()
 
 
-def row_tables(image_lengths, image_dest, image_offset):
-    img_count = image_lengths.shape[1]
-    dp_count = lax.axis_size("dp")
-    fs_count = lax.axis_size("fsdp")
-    dp_index = lax.axis_index("dp")
-    fs_index = lax.axis_index("fsdp")
-    starts = jnp.cumsum(image_lengths, axis=1) - image_lengths
-
-    def group_view(table):
-        return lax.dynamic_index_in_dim(
-            table.reshape(dp_count, fs_count, img_count), fs_index, axis=1, keepdims=False
-        )
-
-    def own(table):
-        return lax.dynamic_index_in_dim(table, dp_index, axis=0, keepdims=False)
-
-    grp_len = group_view(image_lengths) // SLOT
-    grp_start = group_view(starts) // SLOT
-    grp_dest = group_view(image_dest)
-    grp_off = group_view(image_offset) // SLOT
-    own_len, own_start, own_dest, own_off = own(grp_len), own(grp_start), own(grp_dest), own(grp_off)
-    peers = jnp.arange(dp_count, dtype=jnp.int32)
-    unit_count = ROWS // SLOT
-    units = jnp.arange(unit_count, dtype=jnp.int32)
-    arriving = grp_dest == dp_index
-    senders = peers[:, None]
-    back = jnp.sum(jnp.where(arriving & (senders != dp_index), grp_off, 0), axis=1)
-    home_base = jnp.where(own_dest == dp_index, own_off, unit_count + own_dest) - own_start
-    inside = (units[None, :] >= own_start[:, None]) & (units[None, :] < (own_start + own_len)[:, None])
-    home = jnp.sum(jnp.where(inside, home_base[:, None] + units[None, :], 0), axis=0)
-    leaving = (own_dest[None, :] == peers[:, None]) & (own_dest[None, :] != dp_index)
-    send = jnp.sum(jnp.where(leaving, own_start[None, :], 0), axis=1)
-    source_base = jnp.where(senders == dp_index, grp_start, unit_count + senders) - grp_off
-    covers = (
-        arriving[:, :, None]
-        & (units[None, None, :] >= grp_off[:, :, None])
-        & (units[None, None, :] < (grp_off + grp_len)[:, :, None])
-    )
-    place = jnp.sum(
-        jnp.where(covers, source_base[:, :, None] + units[None, None, :], 0), axis=(0, 1)
-    )
-    within = jnp.arange(SLOT, dtype=jnp.int32)
-
-    def unit_rows(first):
-        return (first[:, None] * SLOT + within[None, :]).reshape(-1)
-
-    row_ids = jnp.arange(ROWS, dtype=jnp.int32)
-    image = jnp.sum(jnp.where(row_ids[None, :] >= (own_start * SLOT)[:, None], 1, 0), axis=0)
-    fill = (0, ROWS - dp_count * SLOT)
-    columns = [
-        unit_rows(home),
-        unit_rows(place),
-        image,
-        jnp.pad(unit_rows(back), fill),
-        jnp.pad(unit_rows(send), fill),
-    ]
-    return jnp.stack(columns, axis=1).astype(jnp.int32), image[None, :].astype(jnp.int32)
+def store_kernel(*refs):
+    count = len(refs) // 3
+    sources, targets, buffers = refs[:count], refs[count : 2 * count], refs[2 * count : 3 * count]
+    load_sem, store_sem = refs[-2:]
+    loads, stores = [], []
+    for i, (src, dst, held) in enumerate(zip(sources, targets, buffers)):
+        rows = src.shape[0] // 3
+        for part in range(3):
+            at = pl.ds(part * rows, rows)
+            loads.append(pltpu.make_async_copy(src.at[at], held.at[at], load_sem.at[i, part]))
+            stores.append(pltpu.make_async_copy(held.at[at], dst.at[at], store_sem.at[i, part]))
+    for copy in loads:
+        copy.start()
+    for arrived, copy in zip(loads, stores):
+        arrived.wait()
+        copy.start()
+    for copy in stores:
+        copy.wait()
+
+
+def store(results):
+    any_space = pl.BlockSpec(memory_space=pl.ANY)
+    return pl.pallas_call(
+        store_kernel,
+        out_shape=[jax.ShapeDtypeStruct(result.shape, result.dtype) for result in results],
+        in_specs=[any_space] * len(results),
+        out_specs=[any_space] * len(results),
+        scratch_shapes=[pltpu.VMEM(result.shape, result.dtype) for result in results]
+        + [pltpu.SemaphoreType.DMA((len(results), 3))] * 2,
+        compiler_params=pltpu.CompilerParams(vmem_limit_bytes=63 * 2**20),
+        name="store_results",
+    )(*results)
 
 
 def shards(
     queries, key_vectors, value_vectors, image_lengths, image_dest, image_offset, out_weight, out_grad
 ):
-    table, images = row_tables(image_lengths, image_dest, image_offset)
     any_space = pl.BlockSpec(memory_space=pl.ANY)
     rows = jax.ShapeDtypeStruct((ROWS, D), BF16)
     vmem = pltpu.VMEM
     dma = pltpu.SemaphoreType.DMA
-    return pl.pallas_call(
+    results = pl.pallas_call(
         kernel,
         out_shape=(rows, rows, rows, rows, jax.ShapeDtypeStruct((SHARD, BLOCK), BF16)),
-        in_specs=[pl.BlockSpec(memory_space=vmem)] * 2 + [any_space] * 5,
+        in_specs=[pl.BlockSpec(memory_space=vmem)] + [any_space] * 5,
         out_specs=[any_space] * 5,
         scratch_shapes=[
             vmem((ROWS, D), BF16),
@@ -712,6 +729,7 @@
             *[vmem((3, 4, count, BLOCK), BF16) for _, count, _, _ in PIPES],
             *[vmem((3, count, BLOCK), BF16) for _, count, _, _ in PIPES],
             vmem((SHARD, BLOCK), BF16),
+            vmem((ROWS, HD), jnp.int32),
             dma((5,)),
             dma((3, 4)),
             dma((3, 4)),
@@ -729,7 +747,15 @@
             collective_id=0, has_side_effects=True, vmem_limit_bytes=63 * 2**20
         ),
         name="attention_step",
-    )(table, images, queries, key_vectors, value_vectors, out_weight, out_grad)
+    )(
+        jnp.concatenate([image_lengths, image_dest, image_offset], axis=1),
+        queries,
+        key_vectors,
+        value_vectors,
+        out_weight,
+        out_grad,
+    )
+    return tuple(store(results))
 
 
 def solution(mesh):

time: 139 us -> 129 us (0.928)
  local copies, waits for them, and re-layouts: 14.5 us -> 0.74 us
  Pallas kernels: 121 us -> 127 us
  other arithmetic: 2.48 us -> 0.73 us
    unnamed x13 -> x0, local copies, waits for them, and re-layouts: 9.03 us -> none
    pallas_call x0 -> x1, Pallas kernels: none -> 5.85 us  [store(): pl.pallas_call(store_kernel, out_shape=[jax.ShapeDtypeStruct(result.shape...]
    reshape x4 -> x0, local copies, waits for them, and re-layouts: 2.36 us -> none  [group_view(): table.reshape(dp_count, fs_count, img_count)]
where the time goes in v4:
time: 129 us
  Pallas kernels  127 us (98%)
    pallas_call x1, Pallas kernels, shards(): pl.pallas_call(kernel, out_shape=(rows, rows, rows, rows, jax.ShapeDtypeS...  121 us
    pallas_call x1, Pallas kernels, store(): pl.pallas_call(store_kernel, out_shape=[jax.ShapeDtypeStruct(result.shape...  5.85 us

profile of v4, /device:TPU:1, one launch (start us, length us, event | category | flops | bytes accessed | tf_op | source)
XLA Modules:
  0.0 128.8 jit_solution(15041792081715871463)
XLA Ops:
  0.6 0.7 pad_add_fusion
  1.4 0.7 copy.16.images
  2.1 120.7 %attention_step.1 = (bf16[288,3072]{1,0:T(8,128)(2,1)}, bf16[288,3072]{1,0:T(8,128)(2,1)}, bf16[288,3072]{1,0:T(8,128)(2,1)}, bf16[288,3072]{1,0:T(8,128)(2,1)}, bf16[192,384]{1,0:T(8,128)(2,1)}) custom-call(s32[128,18]{1,0:T(8,128)} %copy.16.images, bf16[288,3072]{1,0:T(8,128)(2,1)} %q_hbm.1, bf16[288,3072]{1,0:T(8,128)(2,1)} %k_hbm.1, ...), custom_call_target="tpu_custom_call" | custom-call | tf_op jit(solution)/shard_map/attention_step/pallas_call | solution.py:699
  122.8 5.8 %store_results.1 = (bf16[288,3072]{1,0:T(8,128)(2,1)}, bf16[288,3072]{1,0:T(8,128)(2,1)}, bf16[288,3072]{1,0:T(8,128)(2,1)}, bf16[288,3072]{1,0:T(8,128)(2,1)}, bf16[192,384]{1,0:T(8,128)(2,1)}) custom-call(bf16[288,3072]{1,0:T(8,128)(2,1)} %get-tuple-element.10.refs_0_, bf16[288,3072]{1,0:T(8,128)(2,1)} %get-tuple-element.11.refs_1_, ...), custom_call_target="tpu_custom_call" | custom-call | tf_op jit(solution)/shard_map/store_results/pallas_call | solution.py:680

commit v5 on v4

--- a/solution.py
+++ b/solution.py
@@ -17,8 +17,10 @@
 SHARD = 192
 CHUNK = 48
 BLOCK = 384
-PIPES = ((0, 64, "zyx", 1), (64, 64, "zxy", 3), (128, 32, "yzx", 1), (160, 32, "yxz", 3))
+PIPES = ((0, 64, "zyx", 1), (64, 48, "zxy", 3), (112, 48, "yzx", 1), (160, 32, "yxz", 3))
 SCALE = HD ** (-0.5)
+TOGETHER = 2
+WIDE = 512
 
 
 def flip(index, by):
@@ -164,36 +166,53 @@
     def sum_lanes(hit, value):
         return jnp.sum(jnp.where(hit, value, 0), axis=1, keepdims=True)
 
-    length, dest, offset, start = images_of(dp)
     row = lax.broadcasted_iota(jnp.int32, (ROWS, 1), 0)
-    inside = (row >= start) & (row < start + length)
-    table[:, 0:1] = sum_lanes(
-        inside, jnp.where(dest == dp, offset, ROWS + SLOT * dest) - start + row
-    )
-    slot_row = lax.broadcasted_iota(jnp.int32, (8 * SLOT, 1), 0)
-    slot, in_slot = lax.div(slot_row, SLOT), lax.rem(slot_row, SLOT)
-    table[: 8 * SLOT, 3:4] = (
-        sum_lanes((dest == slot) & (dest != dp), start + in_slot + 1) - 1
-    )
-    columns = lax.broadcasted_iota(jnp.int32, (1, ROWS), 1)
-    row_image = jnp.zeros((ROWS, 1), jnp.int32)
-    column_image = jnp.zeros((1, ROWS), jnp.int32)
-    for image in range(1, length.shape[1]):
-        first = start[:, image : image + 1]
-        row_image += jnp.where(row >= first, 1, 0)
-        column_image += jnp.where(columns >= first, 1, 0)
-    bias[...] = jnp.where(row_image == column_image, 0.0, -1e30).astype(F32)
-
     senders = [images_of(sender) for sender in range(8)]
-    length, dest, offset, start = [jnp.concatenate(list(part), axis=1) for part in zip(*senders)]
-    sender = lax.div(lax.broadcasted_iota(jnp.int32, length.shape, 1), width)
-    covers = (dest == dp) & (row >= offset) & (row < offset + length)
-    table[:, 1:2] = sum_lanes(
-        covers, jnp.where(sender == dp, start, ROWS + SLOT * sender) - offset + row
-    )
-    table[: 8 * SLOT, 2:3] = (
-        sum_lanes((sender == slot) & (dest == dp) & (sender != dp), offset + in_slot + 1) - 1
-    )
+    first_rows = lax.broadcasted_iota(jnp.int32, (SLOT, 1), 0) + 1
+    for sender, (_, dest, offset, _) in enumerate(senders):
+        arrives = (dest == dp) & (dp != sender)
+        table[sender * SLOT : (sender + 1) * SLOT, 2:3] = (
+            sum_lanes(arrives, offset + first_rows) - 1
+        )
+
+    pl.semaphore_wait(barrier, len(peers))
+
+    def shard_rows(y_, xl_, chunk):
+        return pl.ds(pl.multiple_of((y_ * 2 + xl_) * SHARD + chunk * CHUNK, CHUNK), CHUNK)
+
+    def w_along_y(by, chunk):
+        via = (1 if chunk < 2 else 3) if by == 2 else 0
+        rows = weight.at[shard_rows(flip(y, via), xl, chunk)]
+        return remote(
+            rows,
+            rows,
+            wy_send.at[by - 1, chunk],
+            wy_recv.at[by - 1, chunk],
+            along_y(4 - via if by == 2 else by),
+        )
+
+    def w_along_x(by, chunk):
+        rows = weight.at[shard_rows(flip(y, by), xl, chunk)]
+        return remote(
+            rows,
+            rows,
+            wx_send.at[by, chunk],
+            wx_recv.at[by, chunk],
+            along_x(1 if chunk % 2 == 0 else 3),
+        )
+
+    def forward(by, chunk):
+        w_along_y(by, chunk).wait_recv()
+        if by == (1 if chunk < 2 else 3):
+            w_along_y(2, chunk).start()
+        w_along_x(by, chunk).start()
+
+    loads[0].wait()
+    for step in range(4):
+        w_along_y(1, step).start()
+        w_along_y(3, 3 - step).start()
+    w_along_x(0, 0).start()
+    w_along_x(0, 3).start()
 
     def pick(column, out_rows, in_rows, dst, dst_core=None):
         chosen = lax.broadcasted_iota(jnp.int32, (out_rows, in_rows), 1) == (
@@ -212,44 +231,6 @@
 
         lax.fori_loop(0, D // GROUP, one_part, 0)
 
-    pl.semaphore_wait(barrier, len(peers))
-
-    def shard_rows(y_, xl_, chunk):
-        return pl.ds(pl.multiple_of((y_ * 2 + xl_) * SHARD + chunk * CHUNK, CHUNK), CHUNK)
-
-    def w_along_y(by, chunk):
-        via = (1 if chunk < 2 else 3) if by == 2 else 0
-        rows = weight.at[shard_rows(flip(y, via), xl, chunk)]
-        return remote(
-            rows,
-            rows,
-            wy_send.at[by - 1, chunk],
-            wy_recv.at[by - 1, chunk],
-            along_y(4 - via if by == 2 else by),
-        )
-
-    def w_along_x(by, chunk):
-        rows = weight.at[shard_rows(flip(y, by), xl, chunk)]
-        return remote(
-            rows,
-            rows,
-            wx_send.at[by, chunk],
-            wx_recv.at[by, chunk],
-            along_x(1 if chunk % 2 == 0 else 3),
-        )
-
-    def forward(by, chunk):
-        w_along_y(by, chunk).wait_recv()
-        if by == (1 if chunk < 2 else 3):
-            w_along_y(2, chunk).start()
-        w_along_x(by, chunk).start()
-
-    loads[0].wait()
-    for step in range(4):
-        w_along_y(1, step).start()
-        w_along_y(3, 3 - step).start()
-        w_along_x(0, step).start()
-
     def unit(index):
         return pl.ds(pl.multiple_of(index * SLOT, SLOT), SLOT)
 
@@ -270,6 +251,33 @@
     proj_slots[unit(dp), :] = own_slot
     for by in range(1, 8):
         slots(by, og_slots, 0).start()
+    w_along_x(0, 1).start()
+    w_along_x(0, 2).start()
+    length, dest, offset, start = [jnp.concatenate(list(part), axis=1) for part in zip(*senders)]
+    sender = lax.div(lax.broadcasted_iota(jnp.int32, length.shape, 1), width)
+    covers = (dest == dp) & (row >= offset) & (row < offset + length)
+    table[:, 1:2] = sum_lanes(
+        covers, jnp.where(sender == dp, start, ROWS + SLOT * sender) - offset + row
+    )
+    own_length, own_dest, own_offset, own_start = images_of(dp)
+    slot_row = lax.broadcasted_iota(jnp.int32, (8 * SLOT, 1), 0)
+    slot, in_slot = lax.div(slot_row, SLOT), lax.rem(slot_row, SLOT)
+    inside = (row >= own_start) & (row < own_start + own_length)
+    table[:, 0:1] = sum_lanes(
+        inside, jnp.where(own_dest == dp, own_offset, ROWS + SLOT * own_dest) - own_start + row
+    )
+    table[: 8 * SLOT, 3:4] = (
+        sum_lanes((own_dest == slot) & (own_dest != dp), own_start + in_slot + 1) - 1
+    )
+    columns = lax.broadcasted_iota(jnp.int32, (1, ROWS), 1)
+    row_image = jnp.zeros((ROWS, 1), jnp.int32)
+    column_image = jnp.zeros((1, ROWS), jnp.int32)
+    for image in range(1, width):
+        first = own_start[:, image : image + 1]
+        row_image += jnp.where(row >= first, 1, 0)
+        column_image += jnp.where(columns >= first, 1, 0)
+    bias[...] = jnp.where(row_image == column_image, 0.0, -1e30).astype(F32)
+
     for copy in loads[2:]:
         copy.wait()
 
@@ -281,41 +289,48 @@
         other = jnp.where(core == 0, second, first)
         return mine, other
 
-    def attn_copy(group):
+    def attn_copy(by):
+        group = flip(y, by)
         return remote(
             attn_out.at[group],
             attn_half.at[core, group],
-            core_send.at[0, group],
-            core_recv.at[0, group],
+            core_send.at[0, by],
+            core_recv.at[0, by],
             partner,
         )
 
-    def attend(group):
-        def one_head(i, carry):
-            head = group * 6 + i
-            cols = head_cols(head)
-            scores = contract(qv[:, cols], kv[:, cols], 1, 1) * SCALE + bias[...]
-            powers = jnp.exp(scores - jnp.max(scores, axis=1, keepdims=True))
-            inverse = 1.0 / jnp.sum(powers, axis=1, keepdims=True)
-            weights = (powers * inverse).astype(BF16)
-            probs[head] = weights
-            heads6[:, head_cols(i)] = contract(weights, vv[:, cols], 1, 0).astype(BF16)
+    def attend(by):
+        group = flip(y, by)
+
+        def some_heads(i, carry):
+            at = [i * TOGETHER + t for t in range(TOGETHER)]
+            cols = [head_cols(group * 6 + n) for n in at]
+            loaded = [(qv[:, c], kv[:, c], vv[:, c]) for c in cols]
+            scores = [contract(q, k, 1, 1) * SCALE + bias[...] for q, k, _ in loaded]
+            powers = [jnp.exp(score - jnp.max(score, axis=1, keepdims=True)) for score in scores]
+            weights = [
+                (power * (1.0 / jnp.sum(power, axis=1, keepdims=True))).astype(BF16)
+                for power in powers
+            ]
+            mixed = [contract(w, v, 1, 0).astype(BF16) for w, (_, _, v) in zip(weights, loaded)]
+            for n, w, attn in zip(at, weights, mixed):
+                probs[group * 6 + n] = w
+                heads6[:, head_cols(n)] = attn
             return carry
 
-        lax.fori_loop(0, 6, one_head, 0)
+        lax.fori_loop(0, 6 // TOGETHER, some_heads, 0)
         for t in range(2):
             first = heads6[:, t * HALF : t * HALF + SHARD]
             second = heads6[:, t * HALF + SHARD : (t + 1) * HALF]
             mine, other = split_cores(first, second)
             attn_half[core, group, :, t * SHARD : (t + 1) * SHARD] = mine
             attn_out[group, :, t * SHARD : (t + 1) * SHARD] = other
-        attn_copy(group).start()
-
-    attend(0)
+        attn_copy(by).start()
+
+    attend(2)
     attend(1)
     forward(1, 0)
     forward(3, 3)
-    attend(2)
 
     for by in range(1, 8):
         slots(by, og_slots, 0).wait_recv()
@@ -328,10 +343,6 @@
     attend(3)
     forward(1, 1)
     forward(3, 2)
-
-    for group in range(4):
-        attn_copy(group).wait_recv()
-        attn_t[group] = attn_half[:, group].reshape(2 * ROWS, HALF).T
     og_copy.wait_recv()
 
     grad_scale = (ROWS * 128) ** (-0.5)
@@ -345,55 +356,55 @@
     nexts = (next_0, next_1, next_2, next_3)
     lasts = (last_0, last_1, last_2, last_3)
 
-    def first_copy(pipe, by, z_):
-        near = PIPES[pipe][3]
-        slot = 0 if by == 2 else 1
-        term, pair = terms[pipe], pairs[pipe].at[slot]
-        if pipe < 2:
-            src, dst = term.at[z_], pair
-        elif pipe == 2:
-            src, dst = term.at[flip(y, by), z_], pair.at[z_]
+    def first_copy(pipe, slot, by):
+        _, _, axes, near = PIPES[pipe]
+        toward = flip(here_on[axes[0]], 2 if slot == 0 else near)
+        term, pair, group = terms[pipe], pairs[pipe], flip(y, by)
+        if pipe == 0:
+            src, dst = term.at[toward, group], pair.at[slot, group]
+        elif pipe == 1:
+            src, dst = term.at[toward, :, group], pair.at[slot, :, group]
         else:
-            src, dst = term.at[flip(y, by), :, z_], pair.at[:, z_]
-        return remote(
-            src, dst, rs_send.at[pipe, slot], rs_recv.at[pipe, slot], along[PIPES[pipe][2][0]](near)
-        )
-
-    def compute_terms(by_z):
-        z_ = flip(z, by_z)
-
-        def one_term(by_xh, carry):
-            xh_ = lax.rem(xh + 1 + by_xh, 2)
-            cols = pl.ds(pl.multiple_of((xh_ * 4 + z_) * BLOCK, BLOCK), BLOCK)
-            grads = og_pair[:, :, cols].reshape(2 * ROWS, BLOCK)
-            for y_ in range(4):
-                term = (contract(attn_t[y_], grads, 1, 0) * grad_scale).astype(BF16)
-                for xl_ in range(2):
-                    x_ = xh_ * 2 + xl_
-                    places = ((z_, y_, x_), (z_, x_, y_), (y_, z_, x_), (y_, x_, z_))
-                    for (first_row, count, _, _), buffer, place in zip(PIPES, terms, places):
-                        at = xl_ * SHARD + first_row
-                        buffer[place] = term[at : at + count]
-            return carry
-
-        lax.fori_loop(0, 2, one_term, 0)
-        for pipe in range(4):
-            near = PIPES[pipe][3]
-            if pipe < 2:
-                if by_z in (2, near):
-                    first_copy(pipe, by_z, z_).start()
-            else:
-                first_copy(pipe, 2, z_).start()
-                first_copy(pipe, near, z_).start()
+            src, dst = term.at[toward], pair.at[slot]
+        sem = slot * 4 + by
+        return remote(src, dst, rs_send.at[pipe, sem], rs_recv.at[pipe, sem], along[axes[0]](near))
+
+    def compute_terms(by):
+        group = flip(y, by)
+        attn_copy(by).wait_recv()
+        attn_t[...] = attn_half[:, group].reshape(2 * ROWS, HALF).T
+        for by_z in (2, 1, 3, 0):
+            z_ = flip(z, by_z)
+
+            columns_of = [
+                pl.ds(pl.multiple_of((xh_ * 4 + z_) * BLOCK, BLOCK), BLOCK) for xh_ in range(2)
+            ]
+            grads = jnp.concatenate(
+                [og_pair[:, :, cols].reshape(2 * ROWS, BLOCK) for cols in columns_of], axis=1
+            )
+            term = (contract(attn_t[...], grads, 1, 0) * grad_scale).astype(BF16)
+            for x_ in range(4):
+                places = ((z_, group, x_), (z_, x_, group), (group, z_, x_), (group, x_, z_))
+                left = (x_ // 2) * BLOCK
+                for (first_row, count, _, _), buffer, place in zip(PIPES, terms, places):
+                    at = (x_ % 2) * SHARD + first_row
+                    buffer[place] = term[at : at + count, left : left + BLOCK]
+            for pipe in range(2):
+                if by_z in (2, PIPES[pipe][3]):
+                    first_copy(pipe, 0 if by_z == 2 else 1, by).start()
+        for pipe in (2, 3):
+            if by in (2, PIPES[pipe][3]):
+                first_copy(pipe, 0 if by == 2 else 1, 0).start()
 
     compute_terms(2)
+    compute_terms(1)
     forward(1, 2)
     forward(3, 1)
-    compute_terms(1)
+    attend(0)
     compute_terms(3)
+    compute_terms(0)
     forward(1, 3)
     forward(3, 0)
-    compute_terms(0)
 
     def grad_copy(by):
         return remote(
@@ -438,27 +449,37 @@
             heads6[:, t * HALF : t * HALF + SHARD] = first
             heads6[:, t * HALF + SHARD : (t + 1) * HALF] = second
 
-        def one_head(i, carry):
-            head = flip(y, by) * 6 + i
-            cols = head_cols(head)
-            grads = heads6[:, head_cols(i)]
-            weights = probs[head]
-            wide = weights.astype(F32)
-            queries, keys = qv[:, cols], kv[:, cols]
-            products = contract(grads, vv[:, cols], 1, 1) * wide
-            total = jnp.sum(products, axis=1, keepdims=True)
-            score_grad = ((products - wide * total) * SCALE).astype(BF16)
-            vv[:, cols] = contract(weights, grads, 0, 0).astype(BF16)
-            qv[:, cols] = contract(score_grad, keys, 1, 0).astype(BF16)
-            kv[:, cols] = contract(score_grad, queries, 0, 0).astype(BF16)
+        def some_heads(i, carry):
+            at = [i * TOGETHER + t for t in range(TOGETHER)]
+            heads = [flip(y, by) * 6 + n for n in at]
+            cols = [head_cols(head) for head in heads]
+            loaded = [
+                (qv[:, c], kv[:, c], vv[:, c], probs[head], heads6[:, head_cols(n)])
+                for c, head, n in zip(cols, heads, at)
+            ]
+            products = [contract(g, v, 1, 1) * w.astype(F32) for _, _, v, w, g in loaded]
+            totals = [jnp.sum(product, axis=1, keepdims=True) for product in products]
+            score_grads = [
+                ((product - entry[3].astype(F32) * total) * SCALE).astype(BF16)
+                for product, total, entry in zip(products, totals, loaded)
+            ]
+            grads = [
+                (
+                    contract(ds, k, 1, 0).astype(BF16),
+                    contract(ds, q, 0, 0).astype(BF16),
+                    contract(w, g, 0, 0).astype(BF16),
+                )
+                for ds, (q, k, _, w, g) in zip(score_grads, loaded)
+            ]
+            for c, (dq, dk, dv) in zip(cols, grads):
+                qv[:, c] = dq
+                kv[:, c] = dk
+                vv[:, c] = dv
             return carry
 
-        lax.fori_loop(0, 6, one_head, 0)
+        lax.fori_loop(0, 6 // TOGETHER, some_heads, 0)
         for which in range(3):
             store_copy(by, which).start()
-
-    def all_of(buffer, sem):
-        return pltpu.make_async_copy(buffer, buffer, sem)
 
     def summed(own, others):
         total = own.astype(F32)
@@ -466,67 +487,79 @@
             total += other.astype(F32)
         return total.astype(BF16)
 
-    def second_copy(pipe, half):
+    def second_copy(pipe, part):
         _, _, axes, near = PIPES[pipe]
-        rows = pl.ds(half * 2, 2)
-        return remote(
-            terms[pipe].at[flip(here_on[axes[0]], 4 - near), rows],
-            quads[pipe].at[rows],
-            rs_send.at[pipe, 2],
-            rs_recv.at[pipe, 2],
+        far = flip(here_on[axes[0]], 4 - near)
+        if pipe == 0:
+            place = (flip(y, part),)
+        elif pipe == 1:
+            place = (slice(None), flip(y, part))
+        else:
+            place = (pl.ds(part * 2, 2),)
+        return remote(
+            terms[pipe].at[(far,) + place],
+            quads[pipe].at[place],
+            rs_send.at[pipe, 8 + part],
+            rs_recv.at[pipe, 8 + part],
             along[axes[0]](4 - near),
         )
 
-    def pipe_second(pipe):
-        term, pair = terms[pipe], pairs[pipe]
-        far = flip(here_on[PIPES[pipe][2][0]], 4 - PIPES[pipe][3])
-        all_of(pair.at[0], rs_recv.at[pipe, 0]).wait()
-        for half in range(2):
-
-            def one_block(i, carry):
-                second, third = half * 2 + lax.div(i, 4), lax.rem(i, 4)
-                term[far, second, third] = summed(
-                    term[far, second, third], [pair[0, second, third]]
-                )
-                return carry
-
-            lax.fori_loop(0, 8, one_block, 0)
-            second_copy(pipe, half).start()
+    def add_to(pipe, first, part, others):
+        term = terms[pipe]
+
+        def one_block(i, carry):
+            if pipe == 0:
+                place = (flip(y, part), i)
+            elif pipe == 1:
+                place = (i, flip(y, part))
+            else:
+                place = (part * 2 + lax.div(i, 4), lax.rem(i, 4))
+            term[(first,) + place] = summed(
+                term[(first,) + place], [other[before + place] for other, before in others]
+            )
+            return carry
+
+        lax.fori_loop(0, 4 if pipe < 2 else 8, one_block, 0)
+
+    def pipe_second(pipe, parts):
+        _, _, axes, near = PIPES[pipe]
+        far = flip(here_on[axes[0]], 4 - near)
+        for part in parts:
+            if pipe < 2 or part == 0:
+                first_copy(pipe, 0, part).wait_recv()
+            add_to(pipe, far, part, [(pairs[pipe], (0,))])
+            second_copy(pipe, part).start()
 
     def third_copy(pipe, by):
         axes = PIPES[pipe][2]
         return remote(
             terms[pipe].at[here_on[axes[0]], flip(here_on[axes[1]], by)],
             nexts[pipe].at[by - 1],
-            rs_send.at[pipe, 2 + by],
-            rs_recv.at[pipe, 2 + by],
+            rs_send.at[pipe, 11 + by],
+            rs_recv.at[pipe, 11 + by],
             along[axes[1]](by),
         )
 
     def pipe_third(pipe):
-        term, pair, quad = terms[pipe], pairs[pipe], quads[pipe]
         own = here_on[PIPES[pipe][2][0]]
-        all_of(pair.at[1], rs_recv.at[pipe, 1]).wait()
-        all_of(quad, rs_recv.at[pipe, 2]).wait()
-
-        def one_block(i, carry):
-            second, third = lax.div(i, 4), lax.rem(i, 4)
-            term[own, second, third] = summed(
-                term[own, second, third], [pair[1, second, third], quad[second, third]]
-            )
-            return carry
-
-        lax.fori_loop(0, 16, one_block, 0)
-        for by in (2, 1, 3):
-            third_copy(pipe, by).start()
+        for part in (2, 1, 3, 0) if pipe < 2 else (0, 1):
+            if pipe < 2 or part == 0:
+                first_copy(pipe, 1, part).wait_recv()
+            second_copy(pipe, part).wait_recv()
+            add_to(pipe, own, part, [(pairs[pipe], (1,)), (quads[pipe], ())])
+            if pipe == 0 and part > 0:
+                third_copy(pipe, part).start()
+        if pipe > 0:
+            for by in (2, 1, 3):
+                third_copy(pipe, by).start()
 
     def fourth_copy(pipe, by):
         axes = PIPES[pipe][2]
         return remote(
             terms[pipe].at[here_on[axes[0]], here_on[axes[1]], flip(here_on[axes[2]], by)],
             lasts[pipe].at[by - 1],
-            rs_send.at[pipe, 5 + by],
-            rs_recv.at[pipe, 5 + by],
+            rs_send.at[pipe, 14 + by],
+            rs_recv.at[pipe, 14 + by],
             along[axes[2]](by),
         )
 
@@ -558,18 +591,19 @@
     attend_back(0)
     forward(2, 0)
     forward(2, 3)
+    pipe_second(0, (2, 1))
+    pipe_second(1, (2, 1))
     attn_grad(1)
     attend_back(1)
     forward(2, 1)
     forward(2, 2)
-    pipe_second(0)
-    pipe_second(1)
+    pipe_second(0, (3, 0))
+    pipe_second(1, (3, 0))
     attn_grad(3)
     attend_back(3)
-    pipe_second(2)
-    pipe_second(3)
+    pipe_second(2, (0, 1))
+    pipe_second(3, (0, 1))
     attn_grad(2)
-
     def part_copy(block):
         return remote(
             part_out.at[block], part_in.at[block], core_send.at[3, block], core_recv.at[3, block],
@@ -577,32 +611,27 @@
         )
 
     def one_block(block, carry):
-        cols = pl.ds(pl.multiple_of(block * BLOCK, BLOCK), BLOCK)
-        total = jnp.zeros((2 * ROWS, BLOCK), F32)
-        for group in range(4):
-            total += contract(
-                attn_half[:, group].reshape(2 * ROWS, HALF),
-                weight[group * HALF : (group + 1) * HALF, cols],
-                1,
-                0,
-            )
-        part[...] = total.reshape(2, ROWS, BLOCK)
+        cols = pl.ds(pl.multiple_of(block * WIDE, WIDE), WIDE)
+        attn = jnp.concatenate(
+            [attn_half[:, group].reshape(2 * ROWS, HALF) for group in range(4)], axis=1
+        )
+        part[...] = contract(attn, weight[:, cols], 1, 0).reshape(2, ROWS, WIDE)
         part_out[block] = part[1 - core].astype(BF16)
         part_copy(block).start()
         pool[:ROWS, cols] = part[core].astype(BF16)
         return carry
 
-    lax.fori_loop(0, 8, one_block, 0)
+    lax.fori_loop(0, D // WIDE, one_block, 0)
 
     def add_block(block, carry):
-        cols = pl.ds(pl.multiple_of(block * BLOCK, BLOCK), BLOCK)
+        cols = pl.ds(pl.multiple_of(block * WIDE, WIDE), WIDE)
         part_copy(block).wait_recv()
         pool[:ROWS, cols] = (
             pool[:ROWS, cols].astype(F32) + part_in[block].astype(F32)
         ).astype(BF16)
         return carry
 
-    lax.fori_loop(0, 8, add_block, 0)
+    lax.fori_loop(0, D // WIDE, add_block, 0)
 
     for by in range(1, 8):
         slots(by, og_slots, 0).wait_send()
@@ -610,10 +639,11 @@
     for by in range(1, 8):
         slots(by, proj_slots, 1).start()
 
+    for pipe in (0, 1, 2, 3):
+        pipe_third(pipe)
     attend_back(2)
-
-    for pipe in (2, 3, 0, 1):
-        pipe_third(pipe)
+    for pipe in (0, 1, 2, 3):
+        pipe_fourth(pipe)
 
     for by in range(1, 8):
         slots(by, proj_slots, 1).wait_recv()
@@ -623,8 +653,6 @@
     proj_copy = pltpu.make_async_copy(og_pair.at[core], proj_hbm, load_sem.at[0])
     proj_copy.start()
 
-    for pipe in (2, 3, 0, 1):
-        pipe_fourth(pipe)
     for pipe in (2, 3, 0, 1):
         pipe_last(pipe)
     dw_copy = pltpu.make_async_copy(dw_rows, dw_hbm, load_sem.at[1])
@@ -639,12 +667,14 @@
         grad_copy(by).wait_send()
     for by in range(1, 8):
         slots(by, proj_slots, 1).wait_send()
-    for block in range(8):
+    for block in range(D // WIDE):
         part_copy(block).wait_send()
     for pipe in range(4):
-        for slot in range(2):
-            all_of(pairs[pipe].at[slot], rs_send.at[pipe, slot]).wait()
-        all_of(quads[pipe], rs_send.at[pipe, 2]).wait()
+        for part in range(4) if pipe < 2 else (0,):
+            first_copy(pipe, 0, part).wait_send()
+            first_copy(pipe, 1, part).wait_send()
+        for part in range(4) if pipe < 2 else (0, 1):
+            second_copy(pipe, part).wait_send()
         for by in (1, 2, 3):
             third_copy(pipe, by).wait_send()
             fourth_copy(pipe, by).wait_send()
@@ -712,16 +742,16 @@
             vmem((2, ROWS, D), BF16),
             vmem((2, 4, ROWS, HALF), BF16),
             vmem((4, ROWS, HALF), BF16),
-            vmem((4, HALF, 2 * ROWS), BF16),
+            vmem((HALF, 2 * ROWS), BF16),
             vmem((24, ROWS, ROWS), BF16),
             vmem((ROWS, ROWS), F32),
             vmem((ROWS, GROUP), BF16),
             vmem((4, ROWS, HALF), BF16),
             vmem((4, ROWS, HALF), BF16),
             vmem((4, ROWS, HALF), BF16),
-            vmem((2, ROWS, BLOCK), F32),
-            vmem((8, ROWS, BLOCK), BF16),
-            vmem((8, ROWS, BLOCK), BF16),
+            vmem((2, ROWS, WIDE), F32),
+            vmem((D // WIDE, ROWS, WIDE), BF16),
+            vmem((D // WIDE, ROWS, WIDE), BF16),
             vmem((8 * SLOT, D), BF16),
             *[vmem((4, 4, 4, count, BLOCK), BF16) for _, count, _, _ in PIPES],
             *[vmem((2, 4, 4, count, BLOCK), BF16) for _, count, _, _ in PIPES],
@@ -740,8 +770,8 @@
             dma((2, 7)),
             dma((4, 8)),
             dma((4, 8)),
-            dma((4, 9)),
-            dma((4, 9)),
+            dma((4, 18)),
+            dma((4, 18)),
         ],
         compiler_params=pltpu.CompilerParams(
             collective_id=0, has_side_effects=True, vmem_limit_bytes=63 * 2**20

time: 129 us -> 121 us (0.938)
  Pallas kernels: 127 us -> 118 us
    pallas_call x1, Pallas kernels: 121 us -> 112 us  [shards(): pl.pallas_call(kernel, out_shape=(rows, rows, rows, rows, jax.ShapeDtypeS...]
where the time goes in v5:
time: 121 us; the launch traced here: 120 us
  Pallas kernels  118 us (98%)
    pallas_call x1, Pallas kernels, shards(): pl.pallas_call(kernel, out_shape=(rows, rows, rows, rows, jax.ShapeDtypeS...  112 us
    pallas_call x1, Pallas kernels, store(): pl.pallas_call(store_kernel, out_shape=[jax.ShapeDtypeStruct(result.shape...  5.85 us

profile of v5, /device:TPU:1, one launch (start us, length us, event | category | flops | bytes accessed | tf_op | source)
XLA Modules:
  0.0 119.8 jit_solution(18273686743199963383)
XLA Ops:
  0.6 0.7 pad_add_fusion
  1.4 0.7 copy.16.images
  2.1 111.7 %attention_step.1 = (bf16[288,3072]{1,0:T(8,128)(2,1)}, bf16[288,3072]{1,0:T(8,128)(2,1)}, bf16[288,3072]{1,0:T(8,128)(2,1)}, bf16[288,3072]{1,0:T(8,128)(2,1)}, bf16[192,384]{1,0:T(8,128)(2,1)}) custom-call(s32[128,18]{1,0:T(8,128)} %copy.16.images, bf16[288,3072]{1,0:T(8,128)(2,1)} %q_hbm.1, bf16[288,3072]{1,0:T(8,128)(2,1)} %k_hbm.1, ...), custom_call_target="tpu_custom_call" | custom-call | tf_op jit(solution)/shard_map/attention_step/pallas_call | solution.py:729
  113.8 5.8 %store_results.1 = (bf16[288,3072]{1,0:T(8,128)(2,1)}, bf16[288,3072]{1,0:T(8,128)(2,1)}, bf16[288,3072]{1,0:T(8,128)(2,1)}, bf16[288,3072]{1,0:T(8,128)(2,1)}, bf16[192,384]{1,0:T(8,128)(2,1)}) custom-call(bf16[288,3072]{1,0:T(8,128)(2,1)} %get-tuple-element.10.refs_0_, bf16[288,3072]{1,0:T(8,128)(2,1)} %get-tuple-element.11.refs_1_, ...), custom_call_target="tpu_custom_call" | custom-call | tf_op jit(solution)/shard_map/store_results/pallas_call | solution.py:710

commit v6 on v5

--- a/solution.py
+++ b/solution.py
@@ -16,9 +16,11 @@
 HALF = 384
 SHARD = 192
 CHUNK = 48
+RELAYED = ((1, 0), (3, 3))
 BLOCK = 384
 PIPES = ((0, 64, "zyx", 1), (64, 48, "zxy", 3), (112, 48, "yzx", 1), (160, 32, "yxz", 3))
 SCALE = HD ** (-0.5)
+LOG2_E = 1.4426950408889634
 TOGETHER = 2
 WIDE = 512
 
@@ -60,6 +62,7 @@
     probs,
     bias,
     heads6,
+    grad_both,
     grad_half,
     grad_out,
     grad_in,
@@ -132,15 +135,23 @@
     here = y * 2 + xl
     loads = [
         pltpu.make_async_copy(
-            w_hbm, weight.at[pl.ds(pl.multiple_of(here * SHARD, SHARD), SHARD)], load_sem.at[0]
+            w_hbm, weight.at[pl.ds(pl.multiple_of(here * SHARD, SHARD), SHARD)], load_sem.at[0, 0]
         ),
-        pltpu.make_async_copy(og_hbm, pool.at[0:ROWS], load_sem.at[1]),
-        pltpu.make_async_copy(q_hbm, qv, load_sem.at[2]),
-        pltpu.make_async_copy(k_hbm, kv, load_sem.at[3]),
-        pltpu.make_async_copy(v_hbm, vv, load_sem.at[4]),
+        pltpu.make_async_copy(og_hbm, pool.at[0:ROWS], load_sem.at[1, 0]),
     ]
+
+    def head_load(which, by):
+        cols = pl.ds(pl.multiple_of(flip(y, by) * GROUP, GROUP), GROUP)
+        src, dst = (q_hbm, k_hbm, v_hbm)[which], (qv, kv, vv)[which]
+        return pltpu.make_async_copy(src.at[:, cols], dst.at[:, cols], load_sem.at[2 + which, by])
+
+    for which in range(3):
+        head_load(which, 2).start()
     for copy in loads:
         copy.start()
+    for by in (1, 3, 0):
+        for which in range(3):
+            head_load(which, by).start()
     barrier = pltpu.get_barrier_semaphore()
     peers = (
         [along_x(by) for by in (1, 2, 3)]
@@ -167,6 +178,48 @@
         return jnp.sum(jnp.where(hit, value, 0), axis=1, keepdims=True)
 
     row = lax.broadcasted_iota(jnp.int32, (ROWS, 1), 0)
+    own_length, own_dest, own_offset, own_start = images_of(dp)
+    columns = lax.broadcasted_iota(jnp.int32, (1, ROWS), 1)
+    row_image = jnp.zeros((ROWS, 1), jnp.int32)
+    column_image = jnp.zeros((1, ROWS), jnp.int32)
+    for image in range(1, width):
+        first = own_start[:, image : image + 1]
+        row_image += jnp.where(row >= first, 1, 0)
+        column_image += jnp.where(columns >= first, 1, 0)
+    bias[...] = jnp.where(row_image == column_image, 0.0, -1e30).astype(F32)
+
+    def head_cols(head):
+        return pl.ds(pl.multiple_of(head * HD, HD), HD)
+
+    def split_cores(first, second):
+        mine = jnp.where(core == 0, first, second)
+        other = jnp.where(core == 0, second, first)
+        return mine, other
+
+    def attend_heads(by):
+        group = flip(y, by)
+        for which in range(3):
+            head_load(which, by).wait()
+
+        def some_heads(i, carry):
+            at = [i * TOGETHER + t for t in range(TOGETHER)]
+            cols = [head_cols(group * 6 + n) for n in at]
+            loaded = [(qv[:, c], kv[:, c], vv[:, c]) for c in cols]
+            scores = [contract(q, k, 1, 1) * (SCALE * LOG2_E) + bias[...] for q, k, _ in loaded]
+            powers = [jnp.exp2(score - jnp.max(score, axis=1, keepdims=True)) for score in scores]
+            weights = [
+                (power * (1.0 / jnp.sum(power, axis=1, keepdims=True))).astype(BF16)
+                for power in powers
+            ]
+            mixed = [contract(w, v, 1, 0).astype(BF16) for w, (_, _, v) in zip(weights, loaded)]
+            for n, w, attn in zip(at, weights, mixed):
+                probs[group * 6 + n] = w
+                heads6[:, head_cols(n)] = attn
+            return carry
+
+        lax.fori_loop(0, 6 // TOGETHER, some_heads, 0)
+
+    attend_heads(2)
     senders = [images_of(sender) for sender in range(8)]
     first_rows = lax.broadcasted_iota(jnp.int32, (SLOT, 1), 0) + 1
     for sender, (_, dest, offset, _) in enumerate(senders):
@@ -192,6 +245,11 @@
         )
 
     def w_along_x(by, chunk):
+        if (by, chunk) in RELAYED:
+            rows = weight.at[shard_rows(y, 1 - xl, chunk)]
+            return remote(
+                rows, rows, wx_send.at[by, chunk], wx_recv.at[by, chunk], along_y(by)
+            )
         rows = weight.at[shard_rows(flip(y, by), xl, chunk)]
         return remote(
             rows,
@@ -205,6 +263,11 @@
         w_along_y(by, chunk).wait_recv()
         if by == (1 if chunk < 2 else 3):
             w_along_y(2, chunk).start()
+        if (by, chunk) not in RELAYED:
+            w_along_x(by, chunk).start()
+
+    def relay(by, chunk):
+        w_along_x(0, chunk).wait_recv()
         w_along_x(by, chunk).start()
 
     loads[0].wait()
@@ -214,7 +277,7 @@
     w_along_x(0, 0).start()
     w_along_x(0, 3).start()
 
-    def pick(column, out_rows, in_rows, dst, dst_core=None):
+    def pick(column, out_rows, in_rows, dst, dst_core=None, then=None):
         chosen = lax.broadcasted_iota(jnp.int32, (out_rows, in_rows), 1) == (
             table[:out_rows, column : column + 1]
         )
@@ -227,6 +290,8 @@
                 dst[:, cols] = rows
             else:
                 dst[dst_core, :, cols] = rows
+            if then is not None:
+                then(i).start()
             return carry
 
         lax.fori_loop(0, D // GROUP, one_part, 0)
@@ -259,7 +324,6 @@
     table[:, 1:2] = sum_lanes(
         covers, jnp.where(sender == dp, start, ROWS + SLOT * sender) - offset + row
     )
-    own_length, own_dest, own_offset, own_start = images_of(dp)
     slot_row = lax.broadcasted_iota(jnp.int32, (8 * SLOT, 1), 0)
     slot, in_slot = lax.div(slot_row, SLOT), lax.rem(slot_row, SLOT)
     inside = (row >= own_start) & (row < own_start + own_length)
@@ -269,25 +333,7 @@
     table[: 8 * SLOT, 3:4] = (
         sum_lanes((own_dest == slot) & (own_dest != dp), own_start + in_slot + 1) - 1
     )
-    columns = lax.broadcasted_iota(jnp.int32, (1, ROWS), 1)
-    row_image = jnp.zeros((ROWS, 1), jnp.int32)
-    column_image = jnp.zeros((1, ROWS), jnp.int32)
-    for image in range(1, width):
-        first = own_start[:, image : image + 1]
-        row_image += jnp.where(row >= first, 1, 0)
-        column_image += jnp.where(columns >= first, 1, 0)
-    bias[...] = jnp.where(row_image == column_image, 0.0, -1e30).astype(F32)
-
-    for copy in loads[2:]:
-        copy.wait()
-
-    def head_cols(head):
-        return pl.ds(pl.multiple_of(head * HD, HD), HD)
-
-    def split_cores(first, second):
-        mine = jnp.where(core == 0, first, second)
-        other = jnp.where(core == 0, second, first)
-        return mine, other
+
 
     def attn_copy(by):
         group = flip(y, by)
@@ -299,26 +345,8 @@
             partner,
         )
 
-    def attend(by):
+    def attend_send(by):
         group = flip(y, by)
-
-        def some_heads(i, carry):
-            at = [i * TOGETHER + t for t in range(TOGETHER)]
-            cols = [head_cols(group * 6 + n) for n in at]
-            loaded = [(qv[:, c], kv[:, c], vv[:, c]) for c in cols]
-            scores = [contract(q, k, 1, 1) * SCALE + bias[...] for q, k, _ in loaded]
-            powers = [jnp.exp(score - jnp.max(score, axis=1, keepdims=True)) for score in scores]
-            weights = [
-                (power * (1.0 / jnp.sum(power, axis=1, keepdims=True))).astype(BF16)
-                for power in powers
-            ]
-            mixed = [contract(w, v, 1, 0).astype(BF16) for w, (_, _, v) in zip(weights, loaded)]
-            for n, w, attn in zip(at, weights, mixed):
-                probs[group * 6 + n] = w
-                heads6[:, head_cols(n)] = attn
-            return carry
-
-        lax.fori_loop(0, 6 // TOGETHER, some_heads, 0)
         for t in range(2):
             first = heads6[:, t * HALF : t * HALF + SHARD]
             second = heads6[:, t * HALF + SHARD : (t + 1) * HALF]
@@ -327,8 +355,14 @@
             attn_out[group, :, t * SHARD : (t + 1) * SHARD] = other
         attn_copy(by).start()
 
-    attend(2)
+    def attend(by):
+        attend_heads(by)
+        attend_send(by)
+
+    attend_send(2)
     attend(1)
+    for by, chunk in RELAYED:
+        relay(by, chunk)
     forward(1, 0)
     forward(3, 3)
 
@@ -413,26 +447,15 @@
 
     def attn_grad(by):
         for chunk in range(4):
-            w_along_x(by, chunk).wait_recv()
+            if by > 0 or chunk not in [relayed for _, relayed in RELAYED]:
+                w_along_x(by, chunk).wait_recv()
         rows = pl.ds(pl.multiple_of(flip(y, by) * HALF, HALF), HALF)
 
-        def one_side(side, carry):
-            owner = lax.rem(1 - core + side, 2)
-            half = contract(og_pair[owner], weight[rows, :], 1, 1).astype(BF16)
-
-            @pl.when(side == 0)
-            def _():
-                grad_out[by] = half
-
-            @pl.when(side == 1)
-            def _():
-                grad_half[by] = half
-
-            return carry
-
-        one_side(0, 0)
+        both = contract(og_pair[...].reshape(2 * ROWS, D), weight[rows, :], 1, 1)
+        grad_both[...] = both.astype(BF16).reshape(2, ROWS, HALF)
+        grad_out[by] = grad_both[1 - core]
         grad_copy(by).start()
-        one_side(1, 0)
+        grad_half[by] = grad_both[core]
 
     def store_copy(by, which):
         cols = pl.ds(pl.multiple_of(flip(y, by) * GROUP, GROUP), GROUP)
@@ -460,13 +483,13 @@
             products = [contract(g, v, 1, 1) * w.astype(F32) for _, _, v, w, g in loaded]
             totals = [jnp.sum(product, axis=1, keepdims=True) for product in products]
             score_grads = [
-                ((product - entry[3].astype(F32) * total) * SCALE).astype(BF16)
+                (product - entry[3].astype(F32) * total).astype(BF16)
                 for product, total, entry in zip(products, totals, loaded)
             ]
             grads = [
                 (
-                    contract(ds, k, 1, 0).astype(BF16),
-                    contract(ds, q, 0, 0).astype(BF16),
+                    (contract(ds, k, 1, 0) * SCALE).astype(BF16),
+                    (contract(ds, q, 0, 0) * SCALE).astype(BF16),
                     contract(w, g, 0, 0).astype(BF16),
                 )
                 for ds, (q, k, _, w, g) in zip(score_grads, loaded)
@@ -588,19 +611,18 @@
         )
 
     attn_grad(0)
-    attend_back(0)
     forward(2, 0)
     forward(2, 3)
     pipe_second(0, (2, 1))
     pipe_second(1, (2, 1))
+    attend_back(0)
     attn_grad(1)
-    attend_back(1)
     forward(2, 1)
     forward(2, 2)
+    attend_back(1)
     pipe_second(0, (3, 0))
     pipe_second(1, (3, 0))
     attn_grad(3)
-    attend_back(3)
     pipe_second(2, (0, 1))
     pipe_second(3, (0, 1))
     attn_grad(2)
@@ -639,6 +661,7 @@
     for by in range(1, 8):
         slots(by, proj_slots, 1).start()
 
+    attend_back(3)
     for pipe in (0, 1, 2, 3):
         pipe_third(pipe)
     attend_back(2)
@@ -649,13 +672,18 @@
         slots(by, proj_slots, 1).wait_recv()
     pool[ROWS:, :] = proj_slots[...]
     og_copy.wait_send()
-    pick(1, ROWS, ROWS + 8 * SLOT, og_pair, core)
-    proj_copy = pltpu.make_async_copy(og_pair.at[core], proj_hbm, load_sem.at[0])
-    proj_copy.start()
+
+    def proj_copy(i):
+        cols = pl.ds(pl.multiple_of(i * GROUP, GROUP), GROUP)
+        return pltpu.make_async_copy(
+            og_pair.at[core, :, cols], proj_hbm.at[:, cols], load_sem.at[0, i]
+        )
+
+    pick(1, ROWS, ROWS + 8 * SLOT, og_pair, core, proj_copy)
 
     for pipe in (2, 3, 0, 1):
         pipe_last(pipe)
-    dw_copy = pltpu.make_async_copy(dw_rows, dw_hbm, load_sem.at[1])
+    dw_copy = pltpu.make_async_copy(dw_rows, dw_hbm, load_sem.at[1, 0])
     dw_copy.start()
 
     for by in range(4):
@@ -681,7 +709,8 @@
     for by in range(4):
         for which in range(3):
             store_copy(by, which).wait()
-    proj_copy.wait()
+    for i in range(D // GROUP):
+        proj_copy(i).wait()
     dw_copy.wait()
 
 
@@ -746,6 +775,7 @@
             vmem((24, ROWS, ROWS), BF16),
             vmem((ROWS, ROWS), F32),
             vmem((ROWS, GROUP), BF16),
+            vmem((2, ROWS, HALF), BF16),
             vmem((4, ROWS, HALF), BF16),
             vmem((4, ROWS, HALF), BF16),
             vmem((4, ROWS, HALF), BF16),
@@ -760,7 +790,7 @@
             *[vmem((3, count, BLOCK), BF16) for _, count, _, _ in PIPES],
             vmem((SHARD, BLOCK), BF16),
             vmem((ROWS, HD), jnp.int32),
-            dma((5,)),
+            dma((5, 4)),
             dma((3, 4)),
             dma((3, 4)),
             dma((3, 4)),

time: 121 us -> 119 us (0.983)
  no operation moved by 1% of the time
where the time goes in v6:
time: 119 us
  Pallas kernels  117 us (98%)
    pallas_call x1, Pallas kernels, shards(): pl.pallas_call(kernel, out_shape=(rows, rows, rows, rows, jax.ShapeDtypeS...  111 us
    pallas_call x1, Pallas kernels, store(): pl.pallas_call(store_kernel, out_shape=[jax.ShapeDtypeStruct(result.shape...  5.85 us

profile of v6, /device:TPU:1, one launch (start us, length us, event | category | flops | bytes accessed | tf_op | source)
XLA Modules:
  0.0 118.9 jit_solution(1660105489077314371)
XLA Ops:
  0.6 0.7 pad_add_fusion
  1.4 0.7 copy.16.images
  2.1 110.7 %attention_step.1 = (bf16[288,3072]{1,0:T(8,128)(2,1)}, bf16[288,3072]{1,0:T(8,128)(2,1)}, bf16[288,3072]{1,0:T(8,128)(2,1)}, bf16[288,3072]{1,0:T(8,128)(2,1)}, bf16[192,384]{1,0:T(8,128)(2,1)}) custom-call(s32[128,18]{1,0:T(8,128)} %copy.16.images, bf16[288,3072]{1,0:T(8,128)(2,1)} %q_hbm.1, bf16[288,3072]{1,0:T(8,128)(2,1)} %k_hbm.1, ...), custom_call_target="tpu_custom_call" | custom-call | tf_op jit(solution)/shard_map/attention_step/pallas_call | solution.py:758
  112.8 5.8 %store_results.1 = (bf16[288,3072]{1,0:T(8,128)(2,1)}, bf16[288,3072]{1,0:T(8,128)(2,1)}, bf16[288,3072]{1,0:T(8,128)(2,1)}, bf16[288,3072]{1,0:T(8,128)(2,1)}, bf16[192,384]{1,0:T(8,128)(2,1)}) custom-call(bf16[288,3072]{1,0:T(8,128)(2,1)} %get-tuple-element.10.refs_0_, bf16[288,3072]{1,0:T(8,128)(2,1)} %get-tuple-element.11.refs_1_, ...), custom_call_target="tpu_custom_call" | custom-call | tf_op jit(solution)/shard_map/store_results/pallas_call | solution.py:739
